TPU v7x, 512 devices: a whole 4x4x16 slice. The times are simulated.
512 devices in a mesh: rep: 64 (over z_lo, x, core), tp: 8 (over z_hi, y).
Axes of the slice: x: 4, y: 4, z: 16 (z_hi: 2, z_lo: 8; z = z_hi * 8 + z_lo), core: 2. Of those that a mesh axis runs over, the one named last changes fastest.
Arguments:
- steps_done: int32 [1], replicated, may hold values from 1000 to 99999
- gate_weight: bfloat16 [64, 704, 2048], P('rep', 'tp'), may hold values from -3 to 3
- up_weight: bfloat16 [64, 704, 2048], P('rep', 'tp'), may hold values from -3 to 3
- down_weight: bfloat16 [64, 704, 2048], P('rep', 'tp'), may hold values from -3 to 3
- gate_momentum: bfloat16 [64, 704, 2048], P('rep', 'tp'), may hold values from -0.099609375 to 0.099609375
- up_momentum: bfloat16 [64, 704, 2048], P('rep', 'tp'), may hold values from -0.099609375 to 0.099609375
- down_momentum: bfloat16 [64, 704, 2048], P('rep', 'tp'), may hold values from -0.099609375 to 0.099609375
- gate_variance: bfloat16 [64, 704, 2048], P('rep', 'tp'), may hold values from 0.0009994507 to 0.0099487305
- up_variance: bfloat16 [64, 704, 2048], P('rep', 'tp'), may hold values from 0.0009994507 to 0.0099487305
- down_variance: bfloat16 [64, 704, 2048], P('rep', 'tp'), may hold values from 0.0009994507 to 0.0099487305
- inputs: bfloat16 [2, 8192, 2048], P(None, 'rep', 'tp'), may hold values from -6 to 6
- cotangent: bfloat16 [2, 8192, 2048], P(None, 'rep', 'tp'), may hold values from -6 to 6
Outputs:
- gate_result: bfloat16 [64, 704, 2048], P('rep', 'tp')
- up_result: bfloat16 [64, 704, 2048], P('rep', 'tp')
- down_result: bfloat16 [64, 704, 2048], P('rep', 'tp')
All inputs are finite; a program needn't handle non-finite values.
Results may differ from a plain program's by a relative error of at most 0.014.
Values may be sent and summed in bfloat16 or wider, within the bound.
No kernel may reach another device: no remote copies, remote signals or barrier semaphores. Data moves between devices by JAX's collectives and lax.ppermute only.
A program may use at most 128 MiB of HBM per device.

v0:
```python
from functools import partial
import math

import jax
import jax.numpy as jnp
from jax import lax
from jax.sharding import PartitionSpec as P

D = 2048
FF = 5632
SPAN = 8
STEPS = 2


rate = 0.2
beta_one = 0.9
beta_two = 0.95
adam_eps = 1e-08
hop_levels = 5


def from_partner(value, axis, bit):
    return lax.ppermute(value, axis, [(i, i ^ 1 << bit) for i in range(lax.axis_size(axis))])


def as_sent(value):

    def short(part):
        return part.astype(jnp.bfloat16) if part.dtype == jnp.float32 else part

    return jax.tree.map(short, value)


def passed_along(value, axis, steps):
    count = lax.axis_size(axis)
    pairs = [(source, (source + steps) % count) for source in range(count)]
    return lax.ppermute(value, axis, pairs)


def contract(left, right, left_dim, right_dim):
    return lax.dot_general(
        left, right, (((left_dim,), (right_dim,)), ((), ())), preferred_element_type=jnp.float32
    )


def adam_update(weight, grad, first, second, count):
    first = beta_one * first + (1.0 - beta_one) * grad
    second = beta_two * second + (1.0 - beta_two) * grad * grad
    fix_one = 1.0 - jnp.power(jnp.float32(beta_one), count)
    fix_two = 1.0 - jnp.power(jnp.float32(beta_two), count)
    step_size = rate * (first / fix_one) / (jnp.sqrt(second / fix_two) + adam_eps)
    return ((weight.astype(jnp.float32) - step_size).astype(jnp.bfloat16), first, second)


def blend(mine, peer):
    return ((mine.astype(jnp.float32) + peer.astype(jnp.float32)) * 0.5).astype(jnp.bfloat16)


def join_columns(pair):
    return (
        lax.all_gather(pair[0], "tp", axis=1, tiled=True),
        lax.all_gather(pair[1], "tp", axis=1, tiled=True),
    )


def join_rows(pair):
    place = lax.axis_index("rep")
    first, second = pair
    for level in range(SPAN.bit_length() - 1):
        other_first, other_second = from_partner((first, second), "rep", level)
        lower = jnp.bitwise_and(jnp.right_shift(place, level), 1) == 0
        first = jnp.where(
            lower,
            jnp.concatenate([first, other_first], 0),
            jnp.concatenate([other_first, first], 0),
        )
        second = jnp.where(
            lower,
            jnp.concatenate([second, other_second], 0),
            jnp.concatenate([other_second, second], 0),
        )
    return (first, second)


def send_all(values, distance):
    return passed_along(
        (as_sent(values[0]), as_sent(values[1]), as_sent(values[2])), "rep", distance
    )


def move_from(values, offset, total, sender):
    if offset == 0:
        return values
    return sender(values, total - offset)


def peer_average(values, level, sender):
    total = lax.axis_size("rep")
    replicas = total // SPAN
    branches = []
    for power in range(hop_levels):
        offset = 2**power % replicas
        branches.append(partial(move_from, offset=offset * SPAN, total=total, sender=sender))
    peers = lax.switch(level, branches, values)
    return jax.tree.map(blend, values, peers)


def local(
    steps_done,
    gate_weight,
    up_weight,
    down_weight,
    gate_momentum,
    up_momentum,
    down_momentum,
    gate_variance,
    up_variance,
    down_variance,
    inputs,
    cotangent,
):
    gate_w, up_w, down_w = (gate_weight[0], up_weight[0], down_weight[0])
    firsts = [m[0].astype(jnp.float32) for m in (gate_momentum, up_momentum, down_momentum)]
    seconds = [v[0].astype(jnp.float32) for v in (gate_variance, up_variance, down_variance)]
    inv_model = 1.0 / math.sqrt(D)
    inv_hidden = 1.0 / math.sqrt(FF)
    for step in range(STEPS):
        count = (steps_done[0] + step + 1).astype(jnp.float32)
        level = (steps_done[0] + step) % hop_levels
        pair = (inputs[step], cotangent[step])
        rows, grads_out = join_rows(join_columns(pair))
        gate = contract(gate_w, rows, 1, 1) * inv_model
        upper = contract(up_w, rows, 1, 1) * inv_model
        sigma = jax.nn.sigmoid(gate)
        hidden = (gate * sigma * upper).astype(jnp.bfloat16)
        back = contract(down_w, grads_out, 1, 1) * inv_hidden
        grad_down = contract(hidden, grads_out, 1, 0) * inv_hidden
        down_new, firsts[2], seconds[2] = adam_update(
            down_w, grad_down, firsts[2], seconds[2], count
        )
        d_gate = (back * upper * sigma * (1.0 + gate * (1.0 - sigma))).astype(jnp.bfloat16)
        d_up = (back * gate * sigma).astype(jnp.bfloat16)
        grad_gate = contract(d_gate, rows, 1, 0) * inv_model
        grad_up = contract(d_up, rows, 1, 0) * inv_model
        gate_new, firsts[0], seconds[0] = adam_update(
            gate_w, grad_gate, firsts[0], seconds[0], count
        )
        up_new, firsts[1], seconds[1] = adam_update(up_w, grad_up, firsts[1], seconds[1], count)
        gate_w, up_w, down_w = peer_average((gate_new, up_new, down_new), level, send_all)
    return (gate_w[None], up_w[None], down_w[None])


def solution(mesh):
    return jax.shard_map(
        local,
        mesh=mesh,
        in_specs=(
            P(),
            P("rep", "tp", None),
            P("rep", "tp", None),
            P("rep", "tp", None),
            P("rep", "tp", None),
            P("rep", "tp", None),
            P("rep", "tp", None),
            P("rep", "tp", None),
            P("rep", "tp", None),
            P("rep", "tp", None),
            P(None, "rep", "tp"),
            P(None, "rep", "tp"),
        ),
        out_specs=(P("rep", "tp", None), P("rep", "tp", None), P("rep", "tp", None)),
        check_vma=False,
    )
```

profile of v0, /device:TPU:1, one launch (start us, length us, event | category | flops | bytes accessed | tf_op | source)
XLA Modules:
  0.0 666.7 jit_solution(14232696293791294922)
XLA Ops:
  0.6 0.9 fusion.50
  1.6 64.7 %all-gather.1 = bf16[1,128,2048]{2,1,0:T(8,128)(2,1)S(1)} all-gather(bf16[1,128,256]{2,1,0:T(8,128)(2,1)S(1)} %get-tuple-element.186), channel_id=3, replica_groups=mesh['rep'=64,'tp'=8] {'tp'}, dimensions={2}, use_global_device_ids=true | all-gather | bytes 589824 | tf_op jit(solution)/shard_map/all_gather | solution.py:61
  66.3 7.8 %collective-permute-start.21 = (bf16[128,2048]{1,0:T(8,128)(2,1)S(1)}, bf16[128,2048]{1,0:T(8,128)(2,1)S(1)}, u32[]{:S(2)}, u32[]{:S(2)}) collective-permute-start(bf16[128,2048]{1,0:T(8,128)(2,1)S(1)} %bitcast.76), channel_id=1, source_target_pairs={{0,8},{8,0},{16,24},{24,16},{32,40},{40,32},{48,56},{56,48},{64,72... | collective-permute-start | bytes 1572872 | tf_op jit(solution)/shard_map/ppermute | solution.py:23
  74.1 1.5 collective-permute-done.21
  75.6 0.2 maximum_select_fusion.9
  75.9 1.9 collective-permute-start.22
  77.8 64.8 %all-gather = bf16[1,128,2048]{2,1,0:T(8,128)(2,1)S(1)} all-gather(bf16[1,128,256]{2,1,0:T(8,128)(2,1)S(1)} %get-tuple-element.184), channel_id=2, replica_groups=mesh['rep'=64,'tp'=8] {'tp'}, dimensions={2}, use_global_device_ids=true | all-gather | bytes 589824 | tf_op jit(solution)/shard_map/all_gather | solution.py:62
  142.6 3.9 collective-permute-start.18
  146.5 70.9 %all-gather.3 = bf16[1,128,2048]{2,1,0:T(8,128)(2,1)S(1)} all-gather(bf16[1,128,256]{2,1,0:T(8,128)(2,1)S(1)} %get-tuple-element.185), channel_id=5, replica_groups=mesh['rep'=64,'tp'=8] {'tp'}, dimensions={2}, use_global_device_ids=true | all-gather | bytes 589824 | tf_op jit(solution)/shard_map/all_gather | solution.py:61
  217.4 3.1 collective-permute-start.27
  220.5 75.6 %all-gather.2 = bf16[1,128,2048]{2,1,0:T(8,128)(2,1)S(1)} all-gather(bf16[1,128,256]{2,1,0:T(8,128)(2,1)S(1)} %get-tuple-element.183), channel_id=4, replica_groups=mesh['rep'=64,'tp'=8] {'tp'}, dimensions={2}, use_global_device_ids=true | all-gather | bytes 589824 | tf_op jit(solution)/shard_map/all_gather | solution.py:62
  296.1 3.5 collective-permute-start.24
  299.7 0.2 maximum_select_fusion.8
  299.9 1.9 collective-permute-start.19
  301.9 3.9 maximum_select_fusion.5
  305.7 5.0 collective-permute-start.23
  310.7 1.6 maximum_select_fusion.11
  312.3 2.2 collective-permute-start.28
  314.6 1.6 maximum_select_fusion.10
  316.1 3.1 collective-permute-start.25
  319.2 7.4 %collective-permute-done.19 = bf16[256,2048]{1,0:T(8,128)(2,1)S(1)} collective-permute-done((bf16[256,2048]{1,0:T(8,128)(2,1)S(1)}, bf16[256,2048]{1,0:T(8,128)(2,1)S(1)}, u32[]{:S(2)}, u32[]{:S(2)}) %collective-permute-start.19) | collective-permute-done | bytes 1048608 | tf_op jit(solution)/shard_map/ppermute | solution.py:23
  326.6 2.5 maximum_select_fusion.4
  329.1 4.6 collective-permute-start.20
  334.5 59.6 %collective-permute-done.28 = bf16[256,2048]{1,0:T(8,128)(2,1)} collective-permute-done((bf16[256,2048]{1,0:T(8,128)(2,1)S(1)}, bf16[256,2048]{1,0:T(8,128)(2,1)}, u32[]{:S(2)}, u32[]{:S(2)}) %collective-permute-start.28) | collective-permute-done | bytes 1048608 | tf_op jit(solution)/shard_map/ppermute | solution.py:23
  394.1 3.8 maximum_select_fusion.7
  397.9 4.6 collective-permute-start.29
  402.5 14.1 %collective-permute-done.25 = bf16[256,2048]{1,0:T(8,128)(2,1)} collective-permute-done((bf16[256,2048]{1,0:T(8,128)(2,1)S(1)}, bf16[256,2048]{1,0:T(8,128)(2,1)}, u32[]{:S(2)}, u32[]{:S(2)}) %collective-permute-start.25) | collective-permute-done | bytes 1048608 | tf_op jit(solution)/shard_map/ppermute | solution.py:23
  416.6 2.4 maximum_select_fusion.6
  419.0 4.8 collective-permute-start.26
  423.8 4.4 fusion
  428.3 0.0 copy-start.3
  428.3 0.0 copy-start.6
  428.3 4.4 fusion.1
  432.7 30.4 %collective-permute-done.20 = bf16[512,2048]{1,0:T(8,128)(2,1)} collective-permute-done((bf16[512,2048]{1,0:T(8,128)(2,1)}, bf16[512,2048]{1,0:T(8,128)(2,1)}, u32[]{:S(2)}, u32[]{:S(2)}) %collective-permute-start.20) | collective-permute-done | bytes 2097184 | tf_op jit(solution)/shard_map/ppermute | solution.py:23
  463.2 6.2 subtract_convert_fusion.3
  469.4 4.7 fusion.2
  474.1 0.0 copy-start.14
  474.1 6.2 subtract_convert_fusion.4
  480.3 6.3 subtract_convert_fusion.5
  486.7 39.0 %conditional.8 = (bf16[88,2048]{1,0:T(8,128)(2,1)}, bf16[88,2048]{1,0:T(8,128)(2,1)}, bf16[88,2048]{1,0:T(8,128)(2,1)}) conditional(s32[]{:T(128)} %clamp.6, (bf16[88,2048]{1,0:T(8,128)(2,1)S(1)}, bf16[88,2048]{1,0:T(8,128)(2,1)S(1)}, bf16[88,2048]{1,0:T(8,128)(2,1)S(1)}) %tuple.128, (bf16[88,2048]{1,0:T(8,128)(2,1)S(1)}, ...), branch_computations={%region_0.1_spmd, %region_1.2_spmd, %region_2.3_spmd, %region_3.4_... | conditional | bytes 4325520
  486.7 10.0 %collective-permute-start.3 = (bf16[88,2048]{1,0:T(8,128)(2,1)S(1)}, bf16[88,2048]{1,0:T(8,128)(2,1)}, u32[]{:S(2)}, u32[]{:S(2)}) collective-permute-start(bf16[88,2048]{1,0:T(8,128)(2,1)S(1)} %get-tuple-element.123), channel_id=1, source_target_pairs={{0,384},{8,392},{16,400},{24,408},{32,416},{40,424},{48,432},{56,4... | collective-permute-start | bytes 1081352 | tf_op jit(solution)/shard_map/cond/branch_1_fun/ppermute | solution.py:37
  496.7 1.9 collective-permute-start.4
  498.6 2.5 collective-permute-start.5
  501.1 9.1 %collective-permute-done.3 = bf16[88,2048]{1,0:T(8,128)(2,1)} collective-permute-done((bf16[88,2048]{1,0:T(8,128)(2,1)S(1)}, bf16[88,2048]{1,0:T(8,128)(2,1)}, u32[]{:S(2)}, u32[]{:S(2)}) %collective-permute-start.3) | collective-permute-done | bytes 360480 | tf_op jit(solution)/shard_map/cond/branch_1_fun/ppermute | solution.py:37
  510.2 7.7 %collective-permute-done.4 = bf16[88,2048]{1,0:T(8,128)(2,1)} collective-permute-done((bf16[88,2048]{1,0:T(8,128)(2,1)S(1)}, bf16[88,2048]{1,0:T(8,128)(2,1)}, u32[]{:S(2)}, u32[]{:S(2)}) %collective-permute-start.4) | collective-permute-done | bytes 360480 | tf_op jit(solution)/shard_map/cond/branch_1_fun/ppermute | solution.py:37
  517.9 7.7 %collective-permute-done.5 = bf16[88,2048]{1,0:T(8,128)(2,1)} collective-permute-done((bf16[88,2048]{1,0:T(8,128)(2,1)S(1)}, bf16[88,2048]{1,0:T(8,128)(2,1)}, u32[]{:S(2)}, u32[]{:S(2)}) %collective-permute-start.5) | collective-permute-done | bytes 360480 | tf_op jit(solution)/shard_map/cond/branch_1_fun/ppermute | solution.py:37
  525.7 5.0 convolution_multiply_fusion.1
  530.7 5.0 convolution_multiply_fusion
  535.8 17.3 %collective-permute-done.26 = bf16[512,2048]{1,0:T(8,128)(2,1)} collective-permute-done((bf16[512,2048]{1,0:T(8,128)(2,1)S(1)}, bf16[512,2048]{1,0:T(8,128)(2,1)}, u32[]{:S(2)}, u32[]{:S(2)}) %collective-permute-start.26) | collective-permute-done | bytes 2097184 | tf_op jit(solution)/shard_map/ppermute | solution.py:23
  553.1 3.9 convolution_multiply_fusion.2
  557.0 0.0 copy-start.1
  557.0 0.0 copy-start.11
  557.0 4.5 subtract_convert_fusion
  561.6 5.8 subtract_convert_fusion.1
  567.4 5.8 subtract_convert_fusion.2
  573.2 89.5 %conditional.9 = (bf16[88,2048]{1,0:T(8,128)(2,1)}, bf16[88,2048]{1,0:T(8,128)(2,1)}, bf16[88,2048]{1,0:T(8,128)(2,1)}) conditional(s32[]{:T(128)} %clamp.7, (bf16[88,2048]{1,0:T(8,128)(2,1)S(1)}, bf16[88,2048]{1,0:T(8,128)(2,1)S(1)}, bf16[88,2048]{1,0:T(8,128)(2,1)S(1)}) %tuple.129, (bf16[88,2048]{1,0:T(8,128)(2,1)S(1)}, ...), branch_computations={%region_5.6_spmd, %region_6.7_spmd, %region_7.8_spmd, %region_8.9_... | conditional | bytes 4325520
  573.2 7.8 %collective-permute-start.15 = (bf16[88,2048]{1,0:T(8,128)(2,1)S(1)}, bf16[88,2048]{1,0:T(8,128)(2,1)}, u32[]{:S(2)}, u32[]{:S(2)}) collective-permute-start(bf16[88,2048]{1,0:T(8,128)(2,1)S(1)} %get-tuple-element.135), channel_id=1, source_target_pairs={{0,256},{8,264},{16,272},{24,280},{32,288},{40,296},{48,304},{56,3... | collective-permute-start | bytes 1081352 | tf_op jit(solution)/shard_map/cond/branch_2_fun/ppermute | solution.py:37
  581.1 1.9 collective-permute-start.16
  583.0 7.3 %collective-permute-start.17 = (bf16[88,2048]{1,0:T(8,128)(2,1)S(1)}, bf16[88,2048]{1,0:T(8,128)(2,1)}, u32[]{:S(2)}, u32[]{:S(2)}) collective-permute-start(bf16[88,2048]{1,0:T(8,128)(2,1)S(1)} %get-tuple-element.137), channel_id=1, source_target_pairs={{0,256},{8,264},{16,272},{24,280},{32,288},{40,296},{48,304},{56,3... | collective-permute-start | bytes 1081352 | tf_op jit(solution)/shard_map/cond/branch_2_fun/ppermute | solution.py:37
  590.3 57.0 %collective-permute-done.15 = bf16[88,2048]{1,0:T(8,128)(2,1)} collective-permute-done((bf16[88,2048]{1,0:T(8,128)(2,1)S(1)}, bf16[88,2048]{1,0:T(8,128)(2,1)}, u32[]{:S(2)}, u32[]{:S(2)}) %collective-permute-start.15) | collective-permute-done | bytes 360480 | tf_op jit(solution)/shard_map/cond/branch_2_fun/ppermute | solution.py:37
  647.2 7.7 %collective-permute-done.16 = bf16[88,2048]{1,0:T(8,128)(2,1)} collective-permute-done((bf16[88,2048]{1,0:T(8,128)(2,1)S(1)}, bf16[88,2048]{1,0:T(8,128)(2,1)}, u32[]{:S(2)}, u32[]{:S(2)}) %collective-permute-start.16) | collective-permute-done | bytes 360480 | tf_op jit(solution)/shard_map/cond/branch_2_fun/ppermute | solution.py:37
  655.0 7.7 %collective-permute-done.17 = bf16[88,2048]{1,0:T(8,128)(2,1)} collective-permute-done((bf16[88,2048]{1,0:T(8,128)(2,1)S(1)}, bf16[88,2048]{1,0:T(8,128)(2,1)}, u32[]{:S(2)}, u32[]{:S(2)}) %collective-permute-start.17) | collective-permute-done | bytes 360480 | tf_op jit(solution)/shard_map/cond/branch_2_fun/ppermute | solution.py:37
  662.7 1.8 fusion.19
  664.5 2.2 fusion.17
  (44 shorter events, 0.1 us)
Async XLA Ops:
  0.6 77.2 %copy-start.2 = (bf16[2,128,256]{2,1,0:T(8,128)(2,1)S(1)}, bf16[2,128,256]{2,1,0:T(8,128)(2,1)}, u32[]{:S(2)}) copy-start(bf16[2,128,256]{2,1,0:T(8,128)(2,1)} %param.33) | copy-start | bytes 393220
  66.3 9.3 %collective-permute-start.21 = (bf16[128,2048]{1,0:T(8,128)(2,1)S(1)}, bf16[128,2048]{1,0:T(8,128)(2,1)S(1)}, u32[]{:S(2)}, u32[]{:S(2)}) collective-permute-start(bf16[128,2048]{1,0:T(8,128)(2,1)S(1)} %bitcast.76), channel_id=1, source_target_pairs={{0,8},{8,0},{16,24},{24,16},{32,40},{40,32},{48,56},{56,48},{64,72... | collective-permute-start | bytes 1572872 | tf_op jit(solution)/shard_map/ppermute | solution.py:23
  75.9 226.0 %collective-permute-start.22 = (bf16[256,2048]{1,0:T(8,128)(2,1)S(1)}, bf16[256,2048]{1,0:T(8,128)(2,1)}, u32[]{:S(2)}, u32[]{:S(2)}) collective-permute-start(bf16[256,2048]{1,0:T(8,128)(2,1)S(1)} %maximum_select_fusion.9), channel_id=1, source_target_pairs={{0,16},{8,24},{16,0},{24,8},{32,48},{40,56},{48,32},{56,40},{64,80... | collective-permute-start | bytes 3145736 | tf_op jit(solution)/shard_map/ppermute | solution.py:23
  142.6 157.0 %collective-permute-start.18 = (bf16[128,2048]{1,0:T(8,128)(2,1)S(1)}, bf16[128,2048]{1,0:T(8,128)(2,1)S(1)}, u32[]{:S(2)}, u32[]{:S(2)}) collective-permute-start(bf16[128,2048]{1,0:T(8,128)(2,1)S(1)} %bitcast.74), channel_id=1, source_target_pairs={{0,8},{8,0},{16,24},{24,16},{32,40},{40,32},{48,56},{56,48},{64,72... | collective-permute-start | bytes 1572872 | tf_op jit(solution)/shard_map/ppermute | solution.py:23
  217.4 93.4 %collective-permute-start.27 = (bf16[128,2048]{1,0:T(8,128)(2,1)S(1)}, bf16[128,2048]{1,0:T(8,128)(2,1)}, u32[]{:S(2)}, u32[]{:S(2)}) collective-permute-start(bf16[128,2048]{1,0:T(8,128)(2,1)S(1)} %bitcast.72), channel_id=1, source_target_pairs={{0,8},{8,0},{16,24},{24,16},{32,40},{40,32},{48,56},{56,48},{64,72... | collective-permute-start | bytes 1572872 | tf_op jit(solution)/shard_map/ppermute | solution.py:23
  296.1 18.4 %collective-permute-start.24 = (bf16[128,2048]{1,0:T(8,128)(2,1)S(1)}, bf16[128,2048]{1,0:T(8,128)(2,1)}, u32[]{:S(2)}, u32[]{:S(2)}) collective-permute-start(bf16[128,2048]{1,0:T(8,128)(2,1)S(1)} %bitcast.70), channel_id=1, source_target_pairs={{0,8},{8,0},{16,24},{24,16},{32,40},{40,32},{48,56},{56,48},{64,72... | collective-permute-start | bytes 1572872 | tf_op jit(solution)/shard_map/ppermute | solution.py:23
  299.9 26.7 %collective-permute-start.19 = (bf16[256,2048]{1,0:T(8,128)(2,1)S(1)}, bf16[256,2048]{1,0:T(8,128)(2,1)S(1)}, u32[]{:S(2)}, u32[]{:S(2)}) collective-permute-start(bf16[256,2048]{1,0:T(8,128)(2,1)S(1)} %maximum_select_fusion.8), channel_id=1, source_target_pairs={{0,16},{8,24},{16,0},{24,8},{32,48},{40,56},{48,32},{56,40},{64,80... | collective-permute-start | bytes 3145736 | tf_op jit(solution)/shard_map/ppermute | solution.py:23
  305.7 118.1 %collective-permute-start.23 = (bf16[512,2048]{1,0:T(8,128)(2,1)}, bf16[512,2048]{1,0:T(8,128)(2,1)}, u32[]{:S(2)}, u32[]{:S(2)}) collective-permute-start(bf16[512,2048]{1,0:T(8,128)(2,1)} %maximum_select_fusion.5), channel_id=1, source_target_pairs={{0,32},{8,40},{16,48},{24,56},{32,0},{40,8},{48,16},{56,24},{64,96... | collective-permute-start | bytes 6291464 | tf_op jit(solution)/shard_map/ppermute | solution.py:23
  312.3 81.8 %collective-permute-start.28 = (bf16[256,2048]{1,0:T(8,128)(2,1)S(1)}, bf16[256,2048]{1,0:T(8,128)(2,1)}, u32[]{:S(2)}, u32[]{:S(2)}) collective-permute-start(bf16[256,2048]{1,0:T(8,128)(2,1)S(1)} %maximum_select_fusion.11), channel_id=1, source_target_pairs={{0,16},{8,24},{16,0},{24,8},{32,48},{40,56},{48,32},{56,40},{64,80... | collective-permute-start | bytes 3145736 | tf_op jit(solution)/shard_map/ppermute | solution.py:23
  316.1 100.5 %collective-permute-start.25 = (bf16[256,2048]{1,0:T(8,128)(2,1)S(1)}, bf16[256,2048]{1,0:T(8,128)(2,1)}, u32[]{:S(2)}, u32[]{:S(2)}) collective-permute-start(bf16[256,2048]{1,0:T(8,128)(2,1)S(1)} %maximum_select_fusion.10), channel_id=1, source_target_pairs={{0,16},{8,24},{16,0},{24,8},{32,48},{40,56},{48,32},{56,40},{64,80... | collective-permute-start | bytes 3145736 | tf_op jit(solution)/shard_map/ppermute | solution.py:23
  329.1 134.1 %collective-permute-start.20 = (bf16[512,2048]{1,0:T(8,128)(2,1)}, bf16[512,2048]{1,0:T(8,128)(2,1)}, u32[]{:S(2)}, u32[]{:S(2)}) collective-permute-start(bf16[512,2048]{1,0:T(8,128)(2,1)} %maximum_select_fusion.4), channel_id=1, source_target_pairs={{0,32},{8,40},{16,48},{24,56},{32,0},{40,8},{48,16},{56,24},{64,96... | collective-permute-start | bytes 6291464 | tf_op jit(solution)/shard_map/ppermute | solution.py:23
  397.9 25.9 %copy-start.5 = (bf16[1,88,2048]{2,1,0:T(8,128)(2,1)S(1)}, bf16[1,88,2048]{2,1,0:T(8,128)(2,1)}, u32[]{:S(2)}) copy-start(bf16[1,88,2048]{2,1,0:T(8,128)(2,1)} %param.23) | copy-start | bytes 1081348
  397.9 127.7 %collective-permute-start.29 = (bf16[512,2048]{1,0:T(8,128)(2,1)}, bf16[512,2048]{1,0:T(8,128)(2,1)}, u32[]{:S(2)}, u32[]{:S(2)}) collective-permute-start(bf16[512,2048]{1,0:T(8,128)(2,1)} %maximum_select_fusion.7), channel_id=1, source_target_pairs={{0,32},{8,40},{16,48},{24,56},{32,0},{40,8},{48,16},{56,24},{64,96... | collective-permute-start | bytes 6291464 | tf_op jit(solution)/shard_map/ppermute | solution.py:23
  419.0 9.3 %copy-start.4 = (bf16[1,88,2048]{2,1,0:T(8,128)(2,1)S(1)}, bf16[1,88,2048]{2,1,0:T(8,128)(2,1)}, u32[]{:S(2)}) copy-start(bf16[1,88,2048]{2,1,0:T(8,128)(2,1)} %param.24) | copy-start | bytes 1081348
  419.0 134.0 %collective-permute-start.26 = (bf16[512,2048]{1,0:T(8,128)(2,1)S(1)}, bf16[512,2048]{1,0:T(8,128)(2,1)}, u32[]{:S(2)}, u32[]{:S(2)}) collective-permute-start(bf16[512,2048]{1,0:T(8,128)(2,1)S(1)} %maximum_select_fusion.6), channel_id=1, source_target_pairs={{0,32},{8,40},{16,48},{24,56},{32,0},{40,8},{48,16},{56,24},{64,96... | collective-permute-start | bytes 6291464 | tf_op jit(solution)/shard_map/ppermute | solution.py:23
  428.3 34.9 %copy-start.3 = (bf16[1,88,2048]{2,1,0:T(8,128)(2,1)S(1)}, bf16[1,88,2048]{2,1,0:T(8,128)(2,1)}, u32[]{:S(2)}) copy-start(bf16[1,88,2048]{2,1,0:T(8,128)(2,1)} %param.25) | copy-start | bytes 1081348
  428.3 34.9 %copy-start.6 = (bf16[1,88,2048]{2,1,0:T(8,128)(2,1)S(1)}, bf16[1,88,2048]{2,1,0:T(8,128)(2,1)}, u32[]{:S(2)}) copy-start(bf16[1,88,2048]{2,1,0:T(8,128)(2,1)} %param.28) | copy-start | bytes 1081348
  428.3 34.9 %copy-start.8 = (bf16[1,88,2048]{2,1,0:T(8,128)(2,1)S(1)}, bf16[1,88,2048]{2,1,0:T(8,128)(2,1)}, u32[]{:S(2)}) copy-start(bf16[1,88,2048]{2,1,0:T(8,128)(2,1)} %param.31) | copy-start | bytes 1081348
  469.4 4.7 copy-start.10
  469.4 4.7 copy-start.12
  474.1 6.2 copy-start.14
  474.1 6.2 copy-start.16
  480.3 45.3 %copy-start = (bf16[88,2048]{1,0:T(8,128)(2,1)}, bf16[88,2048]{1,0:T(8,128)(2,1)S(1)}, u32[]{:S(2)}) copy-start(bf16[88,2048]{1,0:T(8,128)(2,1)S(1)} %get-tuple-element.189) | copy-start | bytes 1081348
  486.7 23.5 %collective-permute-start.3 = (bf16[88,2048]{1,0:T(8,128)(2,1)S(1)}, bf16[88,2048]{1,0:T(8,128)(2,1)}, u32[]{:S(2)}, u32[]{:S(2)}) collective-permute-start(bf16[88,2048]{1,0:T(8,128)(2,1)S(1)} %get-tuple-element.123), channel_id=1, source_target_pairs={{0,384},{8,392},{16,400},{24,408},{32,416},{40,424},{48,432},{56,4... | collective-permute-start | bytes 1081352 | tf_op jit(solution)/shard_map/cond/branch_1_fun/ppermute | solution.py:37
  496.7 21.3 %collective-permute-start.4 = (bf16[88,2048]{1,0:T(8,128)(2,1)S(1)}, bf16[88,2048]{1,0:T(8,128)(2,1)}, u32[]{:S(2)}, u32[]{:S(2)}) collective-permute-start(bf16[88,2048]{1,0:T(8,128)(2,1)S(1)} %get-tuple-element.124), channel_id=1, source_target_pairs={{0,384},{8,392},{16,400},{24,408},{32,416},{40,424},{48,432},{56,4... | collective-permute-start | bytes 1081352 | tf_op jit(solution)/shard_map/cond/branch_1_fun/ppermute | solution.py:37
  498.6 27.0 %collective-permute-start.5 = (bf16[88,2048]{1,0:T(8,128)(2,1)S(1)}, bf16[88,2048]{1,0:T(8,128)(2,1)}, u32[]{:S(2)}, u32[]{:S(2)}) collective-permute-start(bf16[88,2048]{1,0:T(8,128)(2,1)S(1)} %get-tuple-element.125), channel_id=1, source_target_pairs={{0,384},{8,392},{16,400},{24,408},{32,416},{40,424},{48,432},{56,4... | collective-permute-start | bytes 1081352 | tf_op jit(solution)/shard_map/cond/branch_1_fun/ppermute | solution.py:37
  553.0 3.9 copy-start.7
  553.0 3.9 copy-start.9
  553.1 3.9 copy-start.19
  557.0 4.6 copy-start.1
  557.0 4.6 copy-start.11
  557.0 4.5 copy-start.13
  557.0 4.5 copy-start.20
  561.6 5.8 copy-start.15
  561.6 5.8 copy-start.17
  561.6 5.8 copy-start.18
  573.2 74.0 %collective-permute-start.15 = (bf16[88,2048]{1,0:T(8,128)(2,1)S(1)}, bf16[88,2048]{1,0:T(8,128)(2,1)}, u32[]{:S(2)}, u32[]{:S(2)}) collective-permute-start(bf16[88,2048]{1,0:T(8,128)(2,1)S(1)} %get-tuple-element.135), channel_id=1, source_target_pairs={{0,256},{8,264},{16,272},{24,280},{32,288},{40,296},{48,304},{56,3... | collective-permute-start | bytes 1081352 | tf_op jit(solution)/shard_map/cond/branch_2_fun/ppermute | solution.py:37
  581.1 73.9 %collective-permute-start.16 = (bf16[88,2048]{1,0:T(8,128)(2,1)S(1)}, bf16[88,2048]{1,0:T(8,128)(2,1)}, u32[]{:S(2)}, u32[]{:S(2)}) collective-permute-start(bf16[88,2048]{1,0:T(8,128)(2,1)S(1)} %get-tuple-element.136), channel_id=1, source_target_pairs={{0,256},{8,264},{16,272},{24,280},{32,288},{40,296},{48,304},{56,3... | collective-permute-start | bytes 1081352 | tf_op jit(solution)/shard_map/cond/branch_2_fun/ppermute | solution.py:37
  583.0 79.7 %collective-permute-start.17 = (bf16[88,2048]{1,0:T(8,128)(2,1)S(1)}, bf16[88,2048]{1,0:T(8,128)(2,1)}, u32[]{:S(2)}, u32[]{:S(2)}) collective-permute-start(bf16[88,2048]{1,0:T(8,128)(2,1)S(1)} %get-tuple-element.137), channel_id=1, source_target_pairs={{0,256},{8,264},{16,272},{24,280},{32,288},{40,296},{48,304},{56,3... | collective-permute-start | bytes 1081352 | tf_op jit(solution)/shard_map/cond/branch_2_fun/ppermute | solution.py:37
where the time goes:
time: 668 us; the launch traced here: 667 us
  blocking collectives  276 us (41%)
  waiting for transfers between devices  227 us (34%)
  starting transfers between devices  77.8 us (12%)
  matrix products  62.3 us (9%)
  other arithmetic  20.2 us (3%)
    all_gather x2, blocking collectives, join_columns(): lax.all_gather(pair[1], 'tp', axis=1, tiled=True)  140 us
    all_gather x2, blocking collectives, join_columns(): lax.all_gather(pair[0], 'tp', axis=1, tiled=True)  136 us
    ppermute x12, waiting for transfers between devices, from_partner(): lax.ppermute(value, axis, [(i, i ^ 1 << bit) for i in range(lax.axis_size...  130 us
    ppermute x6, waiting for transfers between devices, passed_along(): return lax.ppermute(value, axis, pairs)  97 us
    dot_general x12, matrix products, contract(): lax.dot_general(left, right, (((left_dim,), (right_dim,)), ((), ())), pre...  62.3 us
    ppermute x12, starting transfers between devices, from_partner(): lax.ppermute(value, axis, [(i, i ^ 1 << bit) for i in range(lax.axis_size...  46.4 us
    ppermute x6, starting transfers between devices, passed_along(): return lax.ppermute(value, axis, pairs)  31.4 us
  transfers between devices with their start and end apart: 18, of which 12 were waited for; matrix products, arithmetic and copies ran while one was open for 9% of the time, Pallas kernels for 0%

commit v1 on v0

v1 whole, which is shorter than its diff:
```python
import math

import jax
import jax.numpy as jnp
from jax import lax
from jax.experimental import pallas as pl
from jax.experimental.pallas import tpu as pltpu
from jax.sharding import Mesh, PartitionSpec as P

D = 2048
FF = 5632
STEPS = 2
ROWS = 88
PAD = 96
BLK = 256
TOKB = 128
TOK = 1024
NB = D // BLK

rate = 0.2
beta_one = 0.9
beta_two = 0.95
adam_eps = 1e-08
hop_levels = 5
INV_MODEL = 1.0 / math.sqrt(D)
INV_HIDDEN = 1.0 / math.sqrt(FF)


def dot(left, right, right_dim):
    return lax.dot_general(
        left, right, (((1,), (right_dim,)), ((), ())), preferred_element_type=jnp.float32
    )


def pad_rows(value):
    value = value.astype(jnp.float32)
    return jnp.concatenate(
        [value, jnp.zeros((PAD - ROWS, value.shape[1]), jnp.float32)], 0
    ).astype(jnp.bfloat16)


def step_kernel(step, fix, *refs):
    blended = step > 0
    weights, refs = refs[:3], refs[3:]
    if blended:
        peers, refs = refs[:3], refs[3:]
    firsts, seconds, gathered = refs[:3], refs[3:6], refs[6]
    refs = refs[7:]
    new_w, refs = refs[0], refs[1:]
    if not blended:
        new_m, new_v, refs = refs[0], refs[1], refs[2:]
    x_buf, c_buf, gu_buf, v_buf, d_buf, h_buf, sem = refs

    def fetch(kind, buf):
        copies = []
        for t in range(TOK // TOKB):
            for y in range(NB // 2):
                for z in range(2):
                    copies.append(
                        pltpu.make_async_copy(
                            gathered.at[t * (NB // 2) + y, step, kind, z],
                            buf.at[z * (NB // 2) + y, pl.ds(t * TOKB, TOKB), :],
                            sem.at[kind],
                        )
                    )
        return copies

    x_copies, c_copies = fetch(0, x_buf), fetch(1, c_buf)
    for copy in x_copies:
        copy.start()
    for copy in c_copies:
        copy.start()

    def weight(i, cols):
        mine = weights[i][:, cols].astype(jnp.float32)
        if blended:
            mine = ((mine + peers[i][:, cols].astype(jnp.float32)) * 0.5)
            mine = mine.astype(jnp.bfloat16).astype(jnp.float32)
        return mine

    def prepare(j, _):
        cols = pl.ds(pl.multiple_of(j * BLK, BLK), BLK)
        gu_buf[0:PAD, cols] = pad_rows(weight(0, cols))
        gu_buf[PAD : 2 * PAD, cols] = pad_rows(weight(1, cols))
        v_buf[:, cols] = pad_rows(weight(2, cols))
        return 0

    lax.fori_loop(0, NB, prepare, 0)
    for copy in x_copies:
        copy.wait()
    for copy in c_copies:
        copy.wait()

    def forward(t, _):
        toks = pl.ds(pl.multiple_of(t * 256, 256), 256)
        gu = jnp.zeros((2 * PAD, 256), jnp.float32)
        back = jnp.zeros((PAD, 256), jnp.float32)
        for j in range(NB):
            cols = slice(j * BLK, (j + 1) * BLK)
            gu += dot(gu_buf[:, cols], x_buf[j, toks, :], 1)
        for j in range(NB):
            cols = slice(j * BLK, (j + 1) * BLK)
            back += dot(v_buf[:, cols], c_buf[j, toks, :], 1)
        gate, upper = gu[:PAD] * INV_MODEL, gu[PAD:] * INV_MODEL
        back = back * INV_HIDDEN
        sigma = jax.nn.sigmoid(gate)
        gs = gate * sigma
        h_buf[:, toks] = (gs * upper).astype(jnp.bfloat16)
        d_gate = back * upper * sigma * (1.0 + gate * (1.0 - sigma))
        d_buf[0:PAD, toks] = d_gate.astype(jnp.bfloat16)
        d_buf[PAD : 2 * PAD, toks] = (back * gs).astype(jnp.bfloat16)
        return 0

    lax.fori_loop(0, TOK // 256, forward, 0)
    rate_one, inv_two = fix[0], fix[1]

    def backward(j, _):
        cols = pl.ds(pl.multiple_of(j * BLK, BLK), BLK)
        gu = dot(d_buf[...], x_buf[j], 0) * INV_MODEL
        down = dot(h_buf[...], c_buf[j], 0) * INV_HIDDEN
        for i, grad in enumerate((gu[:ROWS], gu[PAD : PAD + ROWS], down[:ROWS])):
            first = firsts[i][:, cols].astype(jnp.float32)
            second = seconds[i][:, cols].astype(jnp.float32)
            first = beta_one * first + (1.0 - beta_one) * grad
            second = beta_two * second + (1.0 - beta_two) * grad * grad
            change = (first * rate_one) / (jnp.sqrt(second * inv_two) + adam_eps)
            new_w[i, :, cols] = (weight(i, cols) - change).astype(jnp.bfloat16)
            if not blended:
                new_m[i, :, cols] = first
                new_v[i, :, cols] = second
        return 0

    lax.fori_loop(0, NB, backward, 0)


def run_step(step, fix, weights, peers, firsts, seconds, gathered):
    vmem = pl.BlockSpec(memory_space=pltpu.VMEM)
    args = [*weights, *(peers if step else ()), *firsts, *seconds]
    shape = (3, ROWS, D)
    outs = [jax.ShapeDtypeStruct(shape, jnp.bfloat16)]
    if not step:
        outs += [jax.ShapeDtypeStruct(shape, jnp.float32)] * 2
    mults = 6 * ROWS * TOK * D

    def body(*refs):
        step_kernel(step, *refs)

    return pl.pallas_call(
        body,
        out_shape=outs,
        in_specs=[pl.BlockSpec(memory_space=pltpu.SMEM)]
        + [vmem] * len(args)
        + [pl.BlockSpec(memory_space=pl.ANY)],
        out_specs=[vmem] * len(outs),
        scratch_shapes=[
            pltpu.VMEM((NB, TOK, BLK), jnp.bfloat16),
            pltpu.VMEM((NB, TOK, BLK), jnp.bfloat16),
            pltpu.VMEM((2 * PAD, D), jnp.bfloat16),
            pltpu.VMEM((PAD, D), jnp.bfloat16),
            pltpu.VMEM((2 * PAD, TOK), jnp.bfloat16),
            pltpu.VMEM((PAD, TOK), jnp.bfloat16),
            pltpu.SemaphoreType.DMA((2,)),
        ],
        compiler_params=pltpu.CompilerParams(vmem_limit_bytes=48 * 2**20),
        cost_estimate=pl.CostEstimate(
            flops=2 * mults, bytes_accessed=16 * 2**20, transcendentals=ROWS * TOK
        ),
        name="adam_step",
    )(fix, *args, gathered)


def shift_rep(value, hops):
    return lax.ppermute(value, "zl", [((i + hops) % 8, i) for i in range(8)])


def exchange(value, level):
    branches = [lambda v, h=2**p % 8: shift_rep(v, h) if h else v for p in range(hop_levels)]
    return lax.switch(level, branches, value)


def local(steps_done, *arrays):
    weights = [a[0] for a in arrays[0:3]]
    firsts = [a[0] for a in arrays[3:6]]
    seconds = [a[0] for a in arrays[6:9]]
    inputs, cotangent = arrays[9:]
    own = jnp.stack([inputs, cotangent], 1)
    other = lax.ppermute(own, "zh", [(0, 1), (1, 0)])
    low = lax.axis_index("zh") == 0
    both = jnp.stack([jnp.where(low, own, other), jnp.where(low, other, own)], 2)
    gathered = lax.all_gather(both, ("x", "c", "y"), axis=0)
    peers = None
    for step in range(STEPS):
        count = (steps_done[0] + step + 1).astype(jnp.float32)
        level = (steps_done[0] + step) % hop_levels
        fix_one = 1.0 - jnp.power(jnp.float32(beta_one), count)
        fix_two = 1.0 - jnp.power(jnp.float32(beta_two), count)
        fix = jnp.stack([rate / fix_one, 1.0 / fix_two])
        new = run_step(step, fix, weights, peers, firsts, seconds, gathered)
        peer = exchange(new[0], level)
        weights = [new[0][i] for i in range(3)]
        peers = [peer[i] for i in range(3)]
        if step == 0:
            firsts, seconds = [new[1][i] for i in range(3)], [new[2][i] for i in range(3)]
    return tuple(
        ((w.astype(jnp.float32) + p.astype(jnp.float32)) * 0.5).astype(jnp.bfloat16)[None]
        for w, p in zip(weights, peers)
    )


def solution(mesh):
    fine = Mesh(mesh.devices.reshape(8, 4, 2, 2, 4), ("zl", "x", "c", "zh", "y"))
    rep, tp = ("zl", "x", "c"), ("zh", "y")
    weight = P(rep, tp, None)
    return jax.shard_map(
        local,
        mesh=fine,
        in_specs=(P(),) + (weight,) * 9 + (P(None, rep, tp),) * 2,
        out_specs=(weight,) * 3,
        check_vma=False,
    )
```

time: 668 us -> 346 us (0.52)
  blocking collectives: 276 us -> 0 us
  matrix products: 62.3 us -> 0 us
  starting transfers between devices: 77.8 us -> 33 us
  Pallas kernels: 0 us -> 24 us
  local copies, waits for them, and re-layouts: 1.04 us -> 21.6 us
  waiting for transfers between devices: 227 us -> 246 us
  other arithmetic: 20.2 us -> 5.37 us
  between operations: 2.01 us -> 15.2 us
    all_gather x4 -> x0, blocking collectives: 276 us -> none  [the longest x2 140 us: join_columns(): lax.all_gather(pair[1], 'tp', axis=1, tiled=True)]
    all_gather x0 -> x1, waiting for transfers between devices: none -> 106 us  [local(): gathered = lax.all_gather(both, ('x', 'c', 'y'), axis=0)]
    ppermute x18 -> x3, waiting for transfers between devices: 227 us -> 140 us  [the longest x2 134 us: shift_rep(): return lax.ppermute(value, 'zl', [((i + hops) % 8, i) for i in range(8)])]
    dot_general x12 -> x0, matrix products: 62.3 us -> none  [contract(): lax.dot_general(left, right, (((left_dim,), (right_dim,)), ((), ())), pre...]
    ppermute x18 -> x3, starting transfers between devices: 77.8 us -> 33 us  [the longest x2 16.7 us: shift_rep(): return lax.ppermute(value, 'zl', [((i + hops) % 8, i) for i in range(8)])]
    pallas_call x0 -> x2, Pallas kernels: none -> 24 us  [run_step(): pl.pallas_call(body, out_shape=outs, in_specs=[pl.BlockSpec(memory_space=...]
    select_n x8 -> x0, other arithmetic: 16.2 us -> none  [the longest x4 9.48 us: join_rows(): jnp.where(lower, jnp.concatenate([first, other_first], 0), jnp.concatenat...]
    all_gather x0 -> x1, local copies, waits for them, and re-layouts: none -> 14.1 us  [local(): gathered = lax.all_gather(both, ('x', 'c', 'y'), axis=0)]
  transfers between devices with their start and end apart: 18 -> 4, of which waited for: 12 -> 4; matrix products, arithmetic and copies ran while one was open for 9% -> 0% of each run, Pallas kernels for 0% -> 0%
where the time goes in v1:
time: 346 us; the launch traced here: 345 us
  waiting for transfers between devices  246 us (71%)
  starting transfers between devices  33 us (10%)
  Pallas kernels  24 us (7%)
  local copies, waits for them, and re-layouts  21.6 us (6%)
  between operations  15.2 us (4%)
  other arithmetic  5.37 us (2%)
    ppermute x2, waiting for transfers between devices, shift_rep(): return lax.ppermute(value, 'zl', [((i + hops) % 8, i) for i in range(8)])  134 us
    all_gather x1, waiting for transfers between devices, local(): gathered = lax.all_gather(both, ('x', 'c', 'y'), axis=0)  106 us
    pallas_call x2, Pallas kernels, run_step(): pl.pallas_call(body, out_shape=outs, in_specs=[pl.BlockSpec(memory_space=...  24 us
    ppermute x2, starting transfers between devices, shift_rep(): return lax.ppermute(value, 'zl', [((i + hops) % 8, i) for i in range(8)])  16.7 us
    ppermute x1, starting transfers between devices, local(): other = lax.ppermute(own, 'zh', [(0, 1), (1, 0)])  16.3 us
    all_gather x1, local copies, waits for them, and re-layouts, local(): gathered = lax.all_gather(both, ('x', 'c', 'y'), axis=0)  14.1 us
  transfers between devices with their start and end apart: 4, of which 4 were waited for; matrix products, arithmetic and copies ran while one was open for 0% of the time, Pallas kernels for 0%

profile of v1, /device:TPU:1, one launch (start us, length us, event | category | flops | bytes accessed | tf_op | source)
XLA Modules:
  0.0 345.0 jit_solution(11317653350067873590)
XLA Ops:
  7.2 0.0 all-gather.3.cloned.1.call-start
  7.2 1.0 pad_maximum_fusion.1
  8.2 16.3 %collective-permute-start.6 = (bf16[2,2,128,256]{3,2,0,1:T(8,128)(2,1)S(1)}, bf16[2,2,128,256]{3,2,0,1:T(8,128)(2,1)S(1)}, u32[]{:S(2)}, u32[]{:S(2)}) collective-permute-start(bf16[2,2,128,256]{3,2,0,1:T(8,128)(2,1)S(1)} %pad_maximum_fusion.1), channel_id=1, source_target_pairs={{0,4},{4,0},{1,5},{5,1},{2,6},{6,2},{3,7},{7,3},{8,12},{12,8},{9,1... | collective-permute-start | bytes 786440 | tf_op jit(solution)/shard_map/ppermute | solution.py:187
  24.5 5.3 %collective-permute-done.6 = bf16[2,2,128,256]{3,2,0,1:T(8,128)(2,1)S(1)} collective-permute-done((bf16[2,2,128,256]{3,2,0,1:T(8,128)(2,1)S(1)}, bf16[2,2,128,256]{3,2,0,1:T(8,128)(2,1)S(1)}, u32[]{:S(2)}, u32[]{:S(2)}) %collective-permute-start.6) | collective-permute-done | bytes 262176 | tf_op jit(solution)/shard_map/ppermute | solution.py:187
  29.8 1.0 select_bitcast_fusion.1
  30.8 0.8 pad_maximum_fusion
  31.6 0.0 all-gather.3.cloned.1.call-update
  32.6 0.1 pad_maximum_fusion.3.refs_0_
  32.7 0.1 pad_maximum_fusion.2.refs_0_
  32.8 0.0 copy-start
  32.8 0.0 copy-start.1
  32.8 0.0 copy-start.2
  32.8 106.0 %all-gather.3.cloned.1.call-done = bf16[64,2,2,128,256]{4,3,0,1,2:T(8,128)(2,1)} async-done(((bf16[2,2,2,128,256]{4,3,0,1,2:T(8,128)(2,1)}), bf16[64,2,2,128,256]{4,3,0,1,2:T(8,128)(2,1)}) %all-gather.3.cloned.1.call-update) | async-done | bytes 16777232 | tf_op jit(solution)/shard_map/all_gather | solution.py:190
  138.8 0.0 copy-start.3
  138.8 0.0 copy-start.4
  138.8 0.0 copy-start.5
  138.8 0.0 copy-start.6
  138.8 0.0 copy-start.7
  138.8 0.0 copy-start.8
  138.9 14.1 %copy.15 = bf16[64,2,2,128,256]{4,3,2,1,0:T(8,128)(2,1)} copy(bf16[64,2,2,128,256]{4,3,0,1,2:T(8,128)(2,1)} %all-gather.3.cloned.1.call-done) | data formatting | bytes 33554432 | tf_op jit(solution)/shard_map/all_gather | solution.py:190
  153.0 0.0 copy-done
  153.0 0.0 copy-done.1
  153.0 0.0 copy-done.2
  153.0 0.0 copy-done.3
  153.0 0.0 copy-done.4
  153.0 0.0 copy-done.5
  153.0 0.0 copy-done.6
  153.0 0.0 copy-done.7
  153.1 0.0 copy-done.8
  153.1 12.6 %adam_step.2 = (bf16[3,88,2048]{2,1,0:T(8,128)(2,1)S(1)}, f32[3,88,2048]{2,1,0:T(8,128)S(1)}, f32[3,88,2048]{2,1,0:T(8,128)}) custom-call(f32[2]{0:T(128)S(1)} %pad_maximum_fusion.3.refs_0_, bf16[88,2048]{1,0:T(8,128)(2,1)S(1)} %bitcast.51, bf16[88,2048]{1,0:T(8,128)(2,1)S(1)} %bitcast.52, bf16[88,2048]{1,0:T(8,128)(2,1)S(1)} %bitcast.53, ...), custom_call_target="tpu_custom_call" | custom-call | flops 2214592512 | bytes 16777216 | tf_op jit(solution)/shard_map/adam_step/pallas_call | solution.py:148
  165.7 0.1 slice_bitcast_fusion.6
  165.7 55.5 %conditional.2 = (bf16[3,88,2048]{2,1,0:T(8,128)(2,1)}, bf16[1,88,2048]{2,1,0:T(8,128)(2,1)}, bf16[1,88,2048]{2,1,0:T(8,128)(2,1)}, bf16[1,88,2048]{2,1,0:T(8,12...) conditional(s32[]{:T(128)} %clamp.6, ...), branch_computations={%region_0.1_spmd, %region_1.2_spmd, %region_2.3_spmd, %region_3.4_... | conditional | bytes 12976252 | solution.py:178
  165.8 9.3 %collective-permute-start.4 = (bf16[3,88,2048]{2,1,0:T(8,128)(2,1)S(1)}, bf16[3,88,2048]{2,1,0:T(8,128)(2,1)S(1)}, u32[]{:S(2)}, u32[]{:S(2)}) collective-permute-start(bf16[3,88,2048]{2,1,0:T(8,128)(2,1)S(1)} %param.1), channel_id=1, source_target_pairs={{128,0},{192,64},{256,128},{320,192},{384,256},{448,320},{0,384},{... | collective-permute-start | bytes 3244040 | tf_op jit(solution)/shard_map/cond/branch_1_fun/ppermute | solution.py:173
  175.1 41.8 %collective-permute-done.4 = bf16[3,88,2048]{2,1,0:T(8,128)(2,1)S(1)} collective-permute-done((bf16[3,88,2048]{2,1,0:T(8,128)(2,1)S(1)}, bf16[3,88,2048]{2,1,0:T(8,128)(2,1)S(1)}, u32[]{:S(2)}, u32[]{:S(2)}) %collective-permute-start.4) | collective-permute-done | bytes 1081376 | tf_op jit(solution)/shard_map/cond/branch_1_fun/ppermute | solution.py:173
  216.9 0.0 copy-start.10
  216.9 1.1 fusion.1
  218.0 0.3 copy-done.10
  218.3 1.0 copy.75
  219.3 1.0 copy.76
  220.3 1.0 copy.77
  221.3 0.0 copy-start.12
  221.3 0.0 copy-start.14
  221.3 0.0 copy-start.16
  221.3 0.7 copy-done.12
  222.0 0.1 copy-done.14
  222.1 0.1 copy-done.16
  222.2 0.0 copy-start.13
  222.2 0.0 copy-start.15
  222.2 0.0 copy-start.17
  222.2 2.0 slice_bitcast_fusion
  224.3 0.0 copy-done.13
  224.3 0.0 copy-done.15
  224.3 0.0 copy-done.17
  224.3 11.4 %adam_step.3 = bf16[3,88,2048]{2,1,0:T(8,128)(2,1)S(1)} custom-call(f32[2]{0:T(128)S(1)} %pad_maximum_fusion.2.refs_0_, bf16[88,2048]{1,0:T(8,128)(2,1)S(1)} %get-tuple-element.66.refs_1_, bf16[88,2048]{1,0:T(8,128)(2,1)S(1)} %get-tuple-element.65.refs_2_, bf16[88,2048]{1,0:T(8,128)(2,1)S(1)} %get-tuple-element.64.refs_3_, bf16[88,2048]{1,0:T(8,128)(2,1)S(1)} %copy-done.13, ...), custom_call_target="tpu_custom_call" | custom-call | flops 2214592512 | bytes 16777216 | tf_op jit(solution)/shard_map/adam_step/pallas_call | solution.py:148
  235.7 100.0 %conditional.3 = (bf16[3,88,2048]{2,1,0:T(8,128)(2,1)}) conditional(s32[]{:T(128)} %clamp.7, bf16[3,88,2048]{2,1,0:T(8,128)(2,1)S(1)} %adam_step.3, bf16[3,88,2048]{2,1,0:T(8,128)(2,1)S(1)} %adam_step.3, bf16[3,88,2048]{2,1,0:T(8,128)(2,1)S(1)} %adam_step.3, bf16[3,88,2048]{2,1,0:T(8,128)(2,1)S(1)} %adam_step.3, ...), branch_computations={%region_5.6_spmd, %region_6.7_spmd, %region_7.8_spmd, %region_8.9_... | conditional | bytes 4325424 | solution.py:178
  235.8 7.4 %collective-permute-start.2 = (bf16[3,88,2048]{2,1,0:T(8,128)(2,1)S(1)}, bf16[3,88,2048]{2,1,0:T(8,128)(2,1)}, u32[]{:S(2)}, u32[]{:S(2)}) collective-permute-start(bf16[3,88,2048]{2,1,0:T(8,128)(2,1)S(1)} %param.7), channel_id=1, source_target_pairs={{256,0},{320,64},{384,128},{448,192},{0,256},{64,320},{128,384},{1... | collective-permute-start | bytes 3244040 | tf_op jit(solution)/shard_map/cond/branch_2_fun/ppermute | solution.py:173
  243.2 92.6 %collective-permute-done.2 = bf16[3,88,2048]{2,1,0:T(8,128)(2,1)} collective-permute-done((bf16[3,88,2048]{2,1,0:T(8,128)(2,1)S(1)}, bf16[3,88,2048]{2,1,0:T(8,128)(2,1)}, u32[]{:S(2)}, u32[]{:S(2)}) %collective-permute-start.2) | collective-permute-done | bytes 1081376 | tf_op jit(solution)/shard_map/cond/branch_2_fun/ppermute | solution.py:173
  335.7 2.4 multiply_convert_fusion
Async XLA Ops:
  7.2 131.7 %all-gather.3.cloned.1.call-start = ((), (), s32[]{:S(2)}) async-start(), calls=%async_computation | async-start | bytes 17301504 | tf_op jit(solution)/shard_map/all_gather | solution.py:190
  8.2 21.5 %collective-permute-start.6 = (bf16[2,2,128,256]{3,2,0,1:T(8,128)(2,1)S(1)}, bf16[2,2,128,256]{3,2,0,1:T(8,128)(2,1)S(1)}, u32[]{:S(2)}, u32[]{:S(2)}) collective-permute-start(bf16[2,2,128,256]{3,2,0,1:T(8,128)(2,1)S(1)} %pad_maximum_fusion.1), channel_id=1, source_target_pairs={{0,4},{4,0},{1,5},{5,1},{2,6},{6,2},{3,7},{7,3},{8,12},{12,8},{9,1... | collective-permute-start | bytes 786440 | tf_op jit(solution)/shard_map/ppermute | solution.py:187
  32.8 120.2 %copy-start = (bf16[1,88,2048]{2,1,0:T(8,128)(2,1)S(1)}, bf16[1,88,2048]{2,1,0:T(8,128)(2,1)}, u32[]{:S(2)}) copy-start(bf16[1,88,2048]{2,1,0:T(8,128)(2,1)} %param.23) | copy-start | bytes 1081348
  32.8 120.2 %copy-start.1 = (bf16[1,88,2048]{2,1,0:T(8,128)(2,1)S(1)}, bf16[1,88,2048]{2,1,0:T(8,128)(2,1)}, u32[]{:S(2)}) copy-start(bf16[1,88,2048]{2,1,0:T(8,128)(2,1)} %param.24) | copy-start | bytes 1081348
  32.8 120.2 %copy-start.2 = (bf16[1,88,2048]{2,1,0:T(8,128)(2,1)S(1)}, bf16[1,88,2048]{2,1,0:T(8,128)(2,1)}, u32[]{:S(2)}) copy-start(bf16[1,88,2048]{2,1,0:T(8,128)(2,1)} %param.25) | copy-start | bytes 1081348
  138.8 14.2 %copy-start.3 = (bf16[1,88,2048]{2,1,0:T(8,128)(2,1)S(1)}, bf16[1,88,2048]{2,1,0:T(8,128)(2,1)}, u32[]{:S(2)}) copy-start(bf16[1,88,2048]{2,1,0:T(8,128)(2,1)} %param.26) | copy-start | bytes 1081348
  138.8 14.2 %copy-start.4 = (bf16[1,88,2048]{2,1,0:T(8,128)(2,1)S(1)}, bf16[1,88,2048]{2,1,0:T(8,128)(2,1)}, u32[]{:S(2)}) copy-start(bf16[1,88,2048]{2,1,0:T(8,128)(2,1)} %param.27) | copy-start | bytes 1081348
  138.8 14.2 %copy-start.5 = (bf16[1,88,2048]{2,1,0:T(8,128)(2,1)S(1)}, bf16[1,88,2048]{2,1,0:T(8,128)(2,1)}, u32[]{:S(2)}) copy-start(bf16[1,88,2048]{2,1,0:T(8,128)(2,1)} %param.28) | copy-start | bytes 1081348
  138.8 14.2 %copy-start.6 = (bf16[1,88,2048]{2,1,0:T(8,128)(2,1)S(1)}, bf16[1,88,2048]{2,1,0:T(8,128)(2,1)}, u32[]{:S(2)}) copy-start(bf16[1,88,2048]{2,1,0:T(8,128)(2,1)} %param.29) | copy-start | bytes 1081348
  138.8 14.2 %copy-start.7 = (bf16[1,88,2048]{2,1,0:T(8,128)(2,1)S(1)}, bf16[1,88,2048]{2,1,0:T(8,128)(2,1)}, u32[]{:S(2)}) copy-start(bf16[1,88,2048]{2,1,0:T(8,128)(2,1)} %param.30) | copy-start | bytes 1081348
  138.8 14.2 %copy-start.8 = (bf16[1,88,2048]{2,1,0:T(8,128)(2,1)S(1)}, bf16[1,88,2048]{2,1,0:T(8,128)(2,1)}, u32[]{:S(2)}) copy-start(bf16[1,88,2048]{2,1,0:T(8,128)(2,1)} %param.31) | copy-start | bytes 1081348
  165.8 51.2 %collective-permute-start.4 = (bf16[3,88,2048]{2,1,0:T(8,128)(2,1)S(1)}, bf16[3,88,2048]{2,1,0:T(8,128)(2,1)S(1)}, u32[]{:S(2)}, u32[]{:S(2)}) collective-permute-start(bf16[3,88,2048]{2,1,0:T(8,128)(2,1)S(1)} %param.1), channel_id=1, source_target_pairs={{128,0},{192,64},{256,128},{320,192},{384,256},{448,320},{0,384},{... | collective-permute-start | bytes 3244040 | tf_op jit(solution)/shard_map/cond/branch_1_fun/ppermute | solution.py:173
  216.9 1.4 copy-start.10
  221.3 0.7 copy-start.12
  221.3 0.9 copy-start.14
  221.3 1.0 copy-start.16
  222.2 2.0 copy-start.13
  222.2 2.0 copy-start.15
  222.2 2.0 copy-start.17
  235.8 100.0 %collective-permute-start.2 = (bf16[3,88,2048]{2,1,0:T(8,128)(2,1)S(1)}, bf16[3,88,2048]{2,1,0:T(8,128)(2,1)}, u32[]{:S(2)}, u32[]{:S(2)}) collective-permute-start(bf16[3,88,2048]{2,1,0:T(8,128)(2,1)S(1)} %param.7), channel_id=1, source_target_pairs={{256,0},{320,64},{384,128},{448,192},{0,256},{64,320},{128,384},{1... | collective-permute-start | bytes 3244040 | tf_op jit(solution)/shard_map/cond/branch_2_fun/ppermute | solution.py:173
Sparse Core Ops, SparseCore 0:
  31.7 107.0 all-gather.2

commit v2 on v1

v2 whole, which is shorter than its diff:
```python
import math

import jax
import jax.numpy as jnp
from jax import lax
from jax.experimental import pallas as pl
from jax.experimental.pallas import tpu as pltpu
from jax.sharding import Mesh, PartitionSpec as P

D = 2048
FF = 5632
STEPS = 2
ROWS = 88
PAD = 96
BLK = 256
TOKB = 128
TOK = 1024
NB = D // BLK

rate = 0.2
beta_one = 0.9
beta_two = 0.95
adam_eps = 1e-08
hop_levels = 5
INV_MODEL = 1.0 / math.sqrt(D)
INV_HIDDEN = 1.0 / math.sqrt(FF)


def dot(left, right, right_dim):
    return lax.dot_general(
        left, right, (((1,), (right_dim,)), ((), ())), preferred_element_type=jnp.float32
    )


def pad_rows(value):
    value = value.astype(jnp.float32)
    return jnp.concatenate(
        [value, jnp.zeros((PAD - ROWS, value.shape[1]), jnp.float32)], 0
    ).astype(jnp.bfloat16)


def step_kernel(step, blended, pos, fix, *refs):
    weights, refs = refs[:3], refs[3:]
    if blended:
        peers, refs = refs[:3], refs[3:]
    firsts_in, seconds_in, refs = refs[:3], refs[3:6], refs[6:]
    mine, theirs, refs = refs[0], refs[1], refs[2:]
    new_w, refs = refs[:3], refs[3:]
    if not step:
        m_out, v_out, refs = refs[:3], refs[3:6], refs[6:]
    gu_buf, v_buf, d_buf, h_buf, w_buf, refs = *refs[:5], refs[5:]
    if blended:
        p_buf, refs = refs[0], refs[1:]
    m_buf, s_buf, refs = refs[0], refs[1], refs[2:]
    if not step:
        new_m, new_v, refs = refs[0], refs[1], refs[2:]
    sem, out_sem = refs
    core, high = pos[0], pos[1]

    def block(x, y, z, kind):
        parts = []
        for half, source in enumerate((mine, theirs)):
            from_core = core if half == 0 else 1 - core
            near = jnp.where(from_core == 0, x, y)
            far = jnp.where(from_core == 0, y, x)
            parts.append(source[far, near, jnp.where(high == z, 0, 1), kind])
        return jnp.concatenate(parts, 0)

    def whole(sources, buf, which):
        return [
            pltpu.make_async_copy(source, buf.at[i], sem.at[which])
            for i, source in enumerate(sources)
        ]

    tensors = whole(weights, w_buf, 0) + (whole(peers, p_buf, 0) if blended else [])
    moments = whole(firsts_in, m_buf, 1) + whole(seconds_in, s_buf, 1)
    for copy in tensors:
        copy.start()
    for copy in moments:
        copy.start()
    for copy in tensors:
        copy.wait()

    def weight(i, cols):
        mine = w_buf[i, :, cols].astype(jnp.float32)
        if blended:
            mine = (mine + p_buf[i, :, cols].astype(jnp.float32)) * 0.5
            mine = mine.astype(jnp.bfloat16).astype(jnp.float32)
        return mine

    def prepare(j, _):
        cols = pl.ds(pl.multiple_of(j * BLK, BLK), BLK)
        gu_buf[0:PAD, cols] = pad_rows(weight(0, cols))
        gu_buf[PAD : 2 * PAD, cols] = pad_rows(weight(1, cols))
        v_buf[:, cols] = pad_rows(weight(2, cols))
        return 0

    lax.fori_loop(0, NB, prepare, 0)

    def forward(t, _):
        toks = pl.ds(pl.multiple_of(t * 256, 256), 256)
        gu = jnp.zeros((2 * PAD, 256), jnp.float32)
        back = jnp.zeros((PAD, 256), jnp.float32)
        for j in range(NB):
            cols = slice(j * BLK, (j + 1) * BLK)
            gu += dot(gu_buf[:, cols], block(t, j % 4, j // 4, 0), 1)
        for j in range(NB):
            cols = slice(j * BLK, (j + 1) * BLK)
            back += dot(v_buf[:, cols], block(t, j % 4, j // 4, 1), 1)
        gate, upper = gu[:PAD] * INV_MODEL, gu[PAD:] * INV_MODEL
        back = back * INV_HIDDEN
        sigma = jax.nn.sigmoid(gate)
        gs = gate * sigma
        h_buf[:, toks] = (gs * upper).astype(jnp.bfloat16)
        d_gate = back * upper * sigma * (1.0 + gate * (1.0 - sigma))
        d_buf[0:PAD, toks] = d_gate.astype(jnp.bfloat16)
        d_buf[PAD : 2 * PAD, toks] = (back * gs).astype(jnp.bfloat16)
        return 0

    lax.fori_loop(0, TOK // 256, forward, 0)
    rate_one, inv_two = fix[0], fix[1]
    for copy in moments:
        copy.wait()

    def backward(j, _):
        cols = pl.ds(pl.multiple_of(j * BLK, BLK), BLK)
        y, z = j % 4, j // 4
        gu = jnp.zeros((2 * PAD, BLK), jnp.float32)
        down = jnp.zeros((PAD, BLK), jnp.float32)
        for x in range(4):
            toks = slice(x * 256, (x + 1) * 256)
            gu += dot(d_buf[:, toks], block(x, y, z, 0), 0)
            down += dot(h_buf[:, toks], block(x, y, z, 1), 0)
        gu, down = gu * INV_MODEL, down * INV_HIDDEN
        for i, grad in enumerate((gu[:ROWS], gu[PAD : PAD + ROWS], down[:ROWS])):
            first = m_buf[i, :, cols].astype(jnp.float32)
            second = s_buf[i, :, cols].astype(jnp.float32)
            first = beta_one * first + (1.0 - beta_one) * grad
            second = beta_two * second + (1.0 - beta_two) * grad * grad
            change = (first * rate_one) / (jnp.sqrt(second * inv_two) + adam_eps)
            new_w[i][:, cols] = (weight(i, cols) - change).astype(jnp.bfloat16)
            if not step:
                new_m[i, :, cols] = first
                new_v[i, :, cols] = second
                for buf, out in ((new_m, m_out), (new_v, v_out)):
                    pltpu.make_async_copy(
                        buf.at[i, :, cols], out[i].at[:, cols], out_sem
                    ).start()
        return 0

    lax.fori_loop(0, NB, backward, 0)
    if not step:
        for i in range(3):
            for buf, out in ((new_m, m_out), (new_v, v_out)):
                pltpu.make_async_copy(buf.at[i], out[i], out_sem).wait()


def run_step(step, pos, fix, weights, peers, firsts, seconds, gathered):
    smem = pl.BlockSpec(memory_space=pltpu.SMEM)
    vmem = pl.BlockSpec(memory_space=pltpu.VMEM)
    hbm = pl.BlockSpec(memory_space=pltpu.HBM)
    blended = peers is not None
    args = [*weights, *(peers or ()), *firsts, *seconds, *gathered]
    outs = [jax.ShapeDtypeStruct((ROWS, D), jnp.bfloat16)] * 3
    if not step:
        outs += [jax.ShapeDtypeStruct((ROWS, D), jnp.float32)] * 6
    mults = 6 * ROWS * TOK * D
    trio = (3, ROWS, D)

    def body(*refs):
        step_kernel(step, blended, *refs)

    new = pl.pallas_call(
        body,
        out_shape=outs,
        in_specs=[smem, smem] + [hbm] * (len(args) - 2) + [vmem] * 2,
        out_specs=[vmem] * 3 + [hbm] * (len(outs) - 3),
        scratch_shapes=[
            pltpu.VMEM((2 * PAD, D), jnp.bfloat16),
            pltpu.VMEM((PAD, D), jnp.bfloat16),
            pltpu.VMEM((2 * PAD, TOK), jnp.bfloat16),
            pltpu.VMEM((PAD, TOK), jnp.bfloat16),
            pltpu.VMEM(trio, jnp.bfloat16),
        ]
        + ([pltpu.VMEM(trio, jnp.bfloat16)] if blended else [])
        + [pltpu.VMEM(trio, firsts[0].dtype)] * 2
        + ([] if step else [pltpu.VMEM(trio, jnp.float32)] * 2)
        + [pltpu.SemaphoreType.DMA((2,)), pltpu.SemaphoreType.DMA],
        compiler_params=pltpu.CompilerParams(vmem_limit_bytes=32 * 2**20),
        cost_estimate=pl.CostEstimate(
            flops=2 * mults, bytes_accessed=16 * 2**20, transcendentals=ROWS * TOK
        ),
        name="adam_step",
    )(pos, fix, *args)
    return new[:3], new[3:6], new[6:9]


def shift_rep(value, hops):
    return lax.ppermute(value, "zl", [((i + hops) % 8, i) for i in range(8)])


def blend(mine, peer):
    return ((mine.astype(jnp.float32) + peer.astype(jnp.float32)) * 0.5).astype(jnp.bfloat16)


def z_partner(value):
    return lax.ppermute(value, "zh", [(0, 1), (1, 0)])


def ring_gather(value, x_core):
    groups = []
    for core in range(2):
        for k in range(4):
            if core == x_core:
                groups.append([i * 8 + core * 4 + k for i in range(4)])
            else:
                groups.append([k * 8 + core * 4 + i for i in range(4)])
    copies = jnp.broadcast_to(value[None], (4,) + value.shape)
    return lax.all_to_all(copies, ("x", "c", "y"), 0, 0, axis_index_groups=groups)


def core_swap(value):
    return lax.ppermute(value, "c", [(0, 1), (1, 0)])


def corrections(steps_done, step):
    count = (steps_done[0] + step + 1).astype(jnp.float32)
    fix_one = 1.0 - jnp.power(jnp.float32(beta_one), count)
    fix_two = 1.0 - jnp.power(jnp.float32(beta_two), count)
    return jnp.stack([rate / fix_one, 1.0 / fix_two])


def both_steps(power, steps_done, *arrays):
    hops = [2 ** ((power + s) % hop_levels) % 8 for s in range(STEPS)]
    weights = [a[0] for a in arrays[0:3]]
    firsts = [a[0] for a in arrays[3:6]]
    seconds = [a[0] for a in arrays[6:9]]
    inputs, cotangent = arrays[9:]
    pos = jnp.stack([lax.axis_index("c"), lax.axis_index("zh")]).astype(jnp.int32)
    own = [jnp.stack([inputs[s], cotangent[s]]) for s in range(STEPS)]
    other = [z_partner(v) for v in own]
    mine = ring_gather(ring_gather(jnp.stack((own[0], other[0])), 0), 1)
    mine, other[1] = lax.optimization_barrier((mine, other[1]))
    theirs = core_swap(mine)
    part = ring_gather(jnp.stack((own[1], other[1])), 0)
    theirs, part = lax.optimization_barrier((theirs, part))
    fix = corrections(steps_done, 0)
    weights, firsts, seconds = run_step(
        0, pos, fix, weights, None, firsts, seconds, (mine, theirs)
    )
    mine = ring_gather(part, 1)
    peers = None
    if hops[0]:
        peers = [shift_rep(w, hops[0]) for w in weights]
        mine, peers = lax.optimization_barrier((mine, peers))
    else:
        mine, weights = lax.optimization_barrier((mine, weights))
    theirs = core_swap(mine)
    fix = corrections(steps_done, 1)
    weights = run_step(1, pos, fix, weights, peers, firsts, seconds, (mine, theirs))[0]
    if hops[1]:
        weights = [blend(w, shift_rep(w, hops[1])) for w in weights]
    return tuple(w[None] for w in weights)


def local(steps_done, *arrays):
    branches = [
        lambda *operands, power=p: both_steps(power, *operands) for p in range(hop_levels)
    ]
    return lax.switch(steps_done[0] % hop_levels, branches, steps_done, *arrays)


def solution(mesh):
    fine = Mesh(mesh.devices.reshape(8, 4, 2, 2, 4), ("zl", "x", "c", "zh", "y"))
    rep, tp = ("zl", "x", "c"), ("zh", "y")
    weight = P(rep, tp, None)
    return jax.shard_map(
        local,
        mesh=fine,
        in_specs=(P(),) + (weight,) * 9 + (P(None, rep, tp),) * 2,
        out_specs=(weight,) * 3,
        check_vma=False,
    )
```

time: 346 us -> 235 us (0.68)
  waiting for transfers between devices: 246 us -> 71.6 us
  starting transfers between devices: 33 us -> 79.3 us
  blocking collectives: 0 us -> 26.8 us
  between operations: 15.2 us -> 1.29 us
    all_gather x1 -> x0, waiting for transfers between devices: 106 us -> none  [local(): gathered = lax.all_gather(both, ('x', 'c', 'y'), axis=0)]
    ppermute x2 -> x6, waiting for transfers between devices: 134 us -> 47.9 us  [shift_rep(): return lax.ppermute(value, 'zl', [((i + hops) % 8, i) for i in range(8)])]
    all_to_all x0 -> x2, blocking collectives: none -> 26.8 us  [ring_gather(): lax.all_to_all(copies, ('x', 'c', 'y'), 0, 0, axis_index_groups=groups)]
    ppermute x1 -> x4, starting transfers between devices: 16.3 us -> 37.2 us  [the longest x2 28.3 us: z_partner(): return lax.ppermute(value, 'zh', [(0, 1), (1, 0)])]
    ppermute x2 -> x6, starting transfers between devices: 16.7 us -> 32.4 us  [shift_rep(): return lax.ppermute(value, 'zl', [((i + hops) % 8, i) for i in range(8)])]
    all_gather x1 -> x0, local copies, waits for them, and re-layouts: 14.1 us -> none  [local(): gathered = lax.all_gather(both, ('x', 'c', 'y'), axis=0)]
    cond x5 -> x32, local copies, waits for them, and re-layouts: 3.24 us -> 16.7 us
    all_to_all x0 -> x2, waiting for transfers between devices: none -> 12.5 us  [ring_gather(): lax.all_to_all(copies, ('x', 'c', 'y'), 0, 0, axis_index_groups=groups)]
  transfers between devices with their start and end apart: 4 -> 12, of which waited for: 4 -> 9; matrix products, arithmetic and copies ran while one was open for 0% -> 1% of each run, Pallas kernels for 0% -> 5%
where the time goes in v2:
time: 235 us; the launch traced here: 232 us
  starting transfers between devices  79.3 us (34%)
  waiting for transfers between devices  71.6 us (30%)
  blocking collectives  26.8 us (11%)
  Pallas kernels  25.2 us (11%)
  local copies, waits for them, and re-layouts  23 us (10%)
  other arithmetic  2.86 us (1%)
    ppermute x6, waiting for transfers between devices, shift_rep(): return lax.ppermute(value, 'zl', [((i + hops) % 8, i) for i in range(8)])  47.9 us
    ppermute x6, starting transfers between devices, shift_rep(): return lax.ppermute(value, 'zl', [((i + hops) % 8, i) for i in range(8)])  32.4 us
    ppermute x2, starting transfers between devices, z_partner(): return lax.ppermute(value, 'zh', [(0, 1), (1, 0)])  28.3 us
    all_to_all x2, blocking collectives, ring_gather(): lax.all_to_all(copies, ('x', 'c', 'y'), 0, 0, axis_index_groups=groups)  26.8 us
    pallas_call x2, Pallas kernels, run_step(): pl.pallas_call(body, out_shape=outs, in_specs=[smem, smem] + [hbm] * (len...  25.2 us
    cond x32, local copies, waits for them, and re-layouts  16.7 us
    all_to_all x2, waiting for transfers between devices, ring_gather(): lax.all_to_all(copies, ('x', 'c', 'y'), 0, 0, axis_index_groups=groups)  12.5 us
    all_to_all x2, starting transfers between devices, ring_gather(): lax.all_to_all(copies, ('x', 'c', 'y'), 0, 0, axis_index_groups=groups)  9.71 us
  transfers between devices with their start and end apart: 12, of which 9 were waited for; matrix products, arithmetic and copies ran while one was open for 1% of the time, Pallas kernels for 5%

profile of v2, /device:TPU:1, one launch (start us, length us, event | category | flops | bytes accessed | tf_op | source)
XLA Modules:
  0.0 231.8 jit_solution(7584597213013394624)
XLA Ops:
  1.3 230.5 %conditional.1 = (bf16[1,88,2048]{2,1,0:T(8,128)(2,1)}, bf16[1,88,2048]{2,1,0:T(8,128)(2,1)}, bf16[1,88,2048]{2,1,0:T(8,128)(2,1)}) conditional(s32[]{:T(128)} %clamp.3, (s32[1]{0:T(128)}, bf16[1,88,2048]{2,1,0:T(8,128)(2,1)}, bf16[1,88,2048]{2,1,0:T(8,128)(2,1)}, bf16[1,88,2048]{2,1,0:T(8,128)(2,1)}, ...), branch_computations={%region_0.1_spmd, %region_1.2_spmd, %region_2.3_spmd, %region_3.4_... | conditional | flops 4432281600 | bytes 184386784 | solution.py:270
  1.3 1.0 fusion.19
  2.3 16.3 %collective-permute-start = (bf16[2,128,256]{2,1,0:T(8,128)(2,1)S(1)}, bf16[2,128,256]{2,1,0:T(8,128)(2,1)S(1)}, u32[]{:S(2)}, u32[]{:S(2)}) collective-permute-start(bf16[2,128,256]{2,1,0:T(8,128)(2,1)S(1)} %get-tuple-element.293), channel_id=1, source_target_pairs={{0,4},{4,0},{1,5},{5,1},{2,6},{6,2},{3,7},{7,3},{8,12},{12,8},{9,1... | collective-permute-start | bytes 393224 | tf_op jit(solution)/shard_map/cond/branch_0_fun/ppermute | solution.py:207
  18.6 2.6 %collective-permute-done = bf16[2,128,256]{2,1,0:T(8,128)(2,1)S(1)} collective-permute-done((bf16[2,128,256]{2,1,0:T(8,128)(2,1)S(1)}, bf16[2,128,256]{2,1,0:T(8,128)(2,1)S(1)}, u32[]{:S(2)}, u32[]{:S(2)}) %collective-permute-start) | collective-permute-done | bytes 131104 | tf_op jit(solution)/shard_map/cond/branch_0_fun/ppermute | solution.py:207
  21.3 0.1 broadcast_in_dim.47
  21.4 14.6 %all_to_all.80 = bf16[4,2,2,128,256]{4,3,2,1,0:T(8,128)(2,1)S(1)} all-to-all(bf16[4,2,2,128,256]{4,3,2,1,0:T(8,128)(2,1)S(1)} %broadcast_in_dim.47), channel_id=1, replica_groups={{0,16,32,48},{1,17,33,49},{2,18,34,50},{3,19,35,51},{8,9,10,11},{24,25,..., dimensions={0} | all-to-all | bytes 2097152 | tf_op jit(solution)/shard_map/cond/branch_0_fun/all_to_all | solution.py:219
  36.0 2.5 %broadcast_in_dim.48 = bf16[4,4,2,2,128,256]{5,4,3,2,1,0:T(8,128)(2,1)} broadcast(bf16[4,2,2,128,256]{4,3,2,1,0:T(8,128)(2,1)S(1)} %all_to_all.80), dimensions={1,2,3,4,5} | broadcast | bytes 5242880 | tf_op jit(solution)/shard_map/cond/branch_0_fun/broadcast_in_dim | solution.py:218
  38.5 4.9 %all-to-all-start.1 = ((bf16[4,4,2,2,128,256]{5,4,3,2,1,0:T(8,128)(2,1)}), bf16[4,4,2,2,128,256]{5,4,3,2,1,0:T(8,128)(2,1)}, u32[]{:S(2)}, u32[]{:S(2)}) async-start(bf16[4,4,2,2,128,256]{5,4,3,2,1,0:T(8,128)(2,1)} %broadcast_in_dim.48), calls=%async_computation.1 | async-start | bytes 8388608 | tf_op jit(solution)/shard_map/cond/branch_0_fun/all_to_all | solution.py:219
  43.4 12.0 %collective-permute-start.1 = (bf16[2,128,256]{2,1,0:T(8,128)(2,1)S(1)}, bf16[2,128,256]{2,1,0:T(8,128)(2,1)S(1)}, u32[]{:S(2)}, u32[]{:S(2)}) collective-permute-start(bf16[2,128,256]{2,1,0:T(8,128)(2,1)S(1)} %get-tuple-element.287), channel_id=1, source_target_pairs={{0,4},{4,0},{1,5},{5,1},{2,6},{6,2},{3,7},{7,3},{8,12},{12,8},{9,1... | collective-permute-start | bytes 393224 | tf_op jit(solution)/shard_map/cond/branch_0_fun/ppermute | solution.py:207
  55.4 2.4 %collective-permute-done.1 = bf16[2,128,256]{2,1,0:T(8,128)(2,1)S(1)} collective-permute-done((bf16[2,128,256]{2,1,0:T(8,128)(2,1)S(1)}, bf16[2,128,256]{2,1,0:T(8,128)(2,1)S(1)}, u32[]{:S(2)}, u32[]{:S(2)}) %collective-permute-start.1) | collective-permute-done | bytes 131104 | tf_op jit(solution)/shard_map/cond/branch_0_fun/ppermute | solution.py:207
  57.8 12.5 %all-to-all-done.1.refs_11_ = bf16[4,4,2,2,128,256]{5,4,3,2,1,0:T(8,128)(2,1)} async-done(((bf16[4,4,2,2,128,256]{5,4,3,2,1,0:T(8,128)(2,1)}), bf16[4,4,2,2,128,256]{5,4,3,2,1,0:T(8,128)(2,1)}, u32[]{:S(2)}, u32[]{:S(2)}) %all-to-all-start.1) | async-done | bytes 4194336 | tf_op jit(solution)/shard_map/cond/branch_0_fun/all_to_all | solution.py:219
  70.3 5.3 %collective-permute-start.2 = (bf16[4,4,2,2,128,256]{5,4,3,2,1,0:T(8,128)(2,1)}, bf16[4,4,2,2,128,256]{5,4,3,2,1,0:T(8,128)(2,1)S(1)}, u32[]{:S(2)}, u32[]{:S(2)}) collective-permute-start(bf16[4,4,2,2,128,256]{5,4,3,2,1,0:T(8,128)(2,1)} %all-to-all-done.1.refs_11_), channel_id=1, source_target_pairs={{0,8},{8,0},{1,9},{9,1},{2,10},{10,2},{3,11},{11,3},{4,12},{12,4},... | collective-permute-start | bytes 12582920 | tf_op jit(solution)/shard_map/cond/branch_0_fun/ppermute | solution.py:223
  75.7 0.1 broadcast_in_dim.56
  75.8 12.2 %all_to_all.81 = bf16[4,2,2,128,256]{4,3,2,1,0:T(8,128)(2,1)S(1)} all-to-all(bf16[4,2,2,128,256]{4,3,2,1,0:T(8,128)(2,1)S(1)} %broadcast_in_dim.56), channel_id=1, replica_groups={{0,16,32,48},{1,17,33,49},{2,18,34,50},{3,19,35,51},{8,9,10,11},{24,25,..., dimensions={0} | all-to-all | bytes 2097152 | tf_op jit(solution)/shard_map/cond/branch_0_fun/all_to_all | solution.py:219
  88.0 0.0 collective-permute-done.2.refs_12_
  88.0 0.0 copy-start
  88.0 2.0 copy-done
  90.0 2.6 %broadcast_in_dim.76 = bf16[4,4,2,2,128,256]{5,4,3,2,1,0:T(8,128)(2,1)} broadcast(bf16[4,2,2,128,256]{4,3,2,1,0:T(8,128)(2,1)S(1)} %all_to_all.81), dimensions={1,2,3,4,5} | broadcast | bytes 5242880 | tf_op jit(solution)/shard_map/cond/branch_0_fun/broadcast_in_dim | solution.py:218
  92.5 4.9 %all-to-all-start.3 = ((bf16[4,4,2,2,128,256]{5,4,3,2,1,0:T(8,128)(2,1)}), bf16[4,4,2,2,128,256]{5,4,3,2,1,0:T(8,128)(2,1)}, u32[]{:S(2)}, u32[]{:S(2)}) async-start(bf16[4,4,2,2,128,256]{5,4,3,2,1,0:T(8,128)(2,1)} %broadcast_in_dim.76), calls=%async_computation.3 | async-start | bytes 8388608 | tf_op jit(solution)/shard_map/cond/branch_0_fun/all_to_all | solution.py:219
  98.2 0.1 pad_add_fusion.refs_0_
  98.3 0.1 pad_maximum_fusion.5.refs_1_
  98.4 0.0 copy-start.1
  98.4 2.2 copy-done.1
  100.6 12.3 %adam_step.10 = (bf16[88,2048]{1,0:T(8,128)(2,1)S(1)}, bf16[88,2048]{1,0:T(8,128)(2,1)S(1)}, bf16[88,2048]{1,0:T(8,128)(2,1)S(1)}, f32[88,2048]{1,0:T(8,128)S(1)...) custom-call(s32[2]{0:T(128)S(1)} %pad_add_fusion.refs_0_, ...), custom_call_target="tpu_custom_call" | custom-call | flops 2214592512 | bytes 16777216 | tf_op jit(solution)/shard_map/cond/branch_0_fun/adam_step/pallas_call | solution.py:173
  112.8 0.0 copy-start.18
  112.8 0.9 copy-done.18
  113.7 0.0 copy-start.20
  113.7 0.9 copy-done.20
  114.6 9.3 %collective-permute-start.3 = (bf16[88,2048]{1,0:T(8,128)(2,1)S(1)}, bf16[88,2048]{1,0:T(8,128)(2,1)S(1)}, u32[]{:S(2)}, u32[]{:S(2)}) collective-permute-start(bf16[88,2048]{1,0:T(8,128)(2,1)S(1)} %get-tuple-element.135.refs_2_), channel_id=1, source_target_pairs={{64,0},{128,64},{192,128},{256,192},{320,256},{384,320},{448,384},... | collective-permute-start | bytes 1081352 | tf_op jit(solution)/shard_map/cond/branch_0_fun/ppermute | solution.py:199
  123.8 9.3 %collective-permute-start.4 = (bf16[88,2048]{1,0:T(8,128)(2,1)S(1)}, bf16[88,2048]{1,0:T(8,128)(2,1)S(1)}, u32[]{:S(2)}, u32[]{:S(2)}) collective-permute-start(bf16[88,2048]{1,0:T(8,128)(2,1)S(1)} %get-tuple-element.136.refs_3_), channel_id=1, source_target_pairs={{64,0},{128,64},{192,128},{256,192},{320,256},{384,320},{448,384},... | collective-permute-start | bytes 1081352 | tf_op jit(solution)/shard_map/cond/branch_0_fun/ppermute | solution.py:199
  133.2 0.0 copy-start.38
  133.2 0.7 copy-done.38
  133.9 1.9 collective-permute-start.5
  135.8 0.0 copy-start.40
  135.8 0.7 copy-done.40
  136.6 0.0 collective-permute-done.3.refs_5_
  136.6 0.0 copy-start.50
  136.6 0.7 copy-done.50
  137.3 3.5 %collective-permute-done.4.refs_6_ = bf16[88,2048]{1,0:T(8,128)(2,1)S(1)} collective-permute-done((bf16[88,2048]{1,0:T(8,128)(2,1)S(1)}, bf16[88,2048]{1,0:T(8,128)(2,1)S(1)}, u32[]{:S(2)}, u32[]{:S(2)}) %collective-permute-start.4) | collective-permute-done | bytes 360480 | tf_op jit(solution)/shard_map/cond/branch_0_fun/ppermute | solution.py:199
  140.8 0.0 copy-start.56
  140.8 0.7 copy-done.56
  141.5 7.0 %collective-permute-done.5.refs_7_ = bf16[88,2048]{1,0:T(8,128)(2,1)S(1)} collective-permute-done((bf16[88,2048]{1,0:T(8,128)(2,1)S(1)}, bf16[88,2048]{1,0:T(8,128)(2,1)S(1)}, u32[]{:S(2)}, u32[]{:S(2)}) %collective-permute-start.5) | collective-permute-done | bytes 360480 | tf_op jit(solution)/shard_map/cond/branch_0_fun/ppermute | solution.py:199
  148.5 0.7 copy-done.62
  149.2 0.0 all-to-all-done.3.refs_14_
  149.3 3.6 %collective-permute-start.6 = (bf16[4,4,2,2,128,256]{5,4,3,2,1,0:T(8,128)(2,1)}, bf16[4,4,2,2,128,256]{5,4,3,2,1,0:T(8,128)(2,1)S(1)}, u32[]{:S(2)}, u32[]{:S(2)}) collective-permute-start(bf16[4,4,2,2,128,256]{5,4,3,2,1,0:T(8,128)(2,1)} %all-to-all-done.3.refs_14_), channel_id=1, source_target_pairs={{0,8},{8,0},{1,9},{9,1},{2,10},{10,2},{3,11},{11,3},{4,12},{12,4},... | collective-permute-start | bytes 12582920 | tf_op jit(solution)/shard_map/cond/branch_0_fun/ppermute | solution.py:223
  153.7 0.1 pad_maximum_fusion.4.refs_1_
  153.8 6.1 %collective-permute-done.6.refs_15_ = bf16[4,4,2,2,128,256]{5,4,3,2,1,0:T(8,128)(2,1)S(1)} collective-permute-done((bf16[4,4,2,2,128,256]{5,4,3,2,1,0:T(8,128)(2,1)}, bf16[4,4,2,2,128,256]{5,4,3,2,1,0:T(8,128)(2,1)S(1)}, u32[]{:S(2)}, u32[]{:S(2)}) %collective-permute-start.6) | collective-permute-done | bytes 4194336 | tf_op jit(solution)/shard_map/cond/branch_0_fun/ppermute | solution.py:223
  159.8 1.1 copy-done.19
  161.0 1.1 copy-done.21
  162.1 1.0 copy-done.39
  163.0 1.0 copy-done.41
  164.0 1.0 copy-done.51
  165.0 1.0 copy-done.57
  166.0 1.0 copy-done.63
  167.0 12.9 %adam_step.11 = (bf16[88,2048]{1,0:T(8,128)(2,1)S(1)}, bf16[88,2048]{1,0:T(8,128)(2,1)S(1)}, bf16[88,2048]{1,0:T(8,128)(2,1)S(1)}) custom-call(s32[2]{0:T(128)S(1)} %pad_add_fusion.refs_0_, f32[2]{0:T(128)S(1)} %pad_maximum_fusion.4.refs_1_, bf16[88,2048]{1,0:T(8,128)(2,1)S(1)} %get-tuple-element.135.refs_2_, bf16[88,2048]{1,0:T(8,128)(2,1)S(1)} %copy-done.39, ...), custom_call_target="tpu_custom_call" | custom-call | flops 2214592512 | bytes 16777216 | tf_op jit(solution)/shard_map/cond/branch_0_fun/adam_step/pallas_call | solution.py:173
  179.9 8.0 %collective-permute-start.7 = (bf16[88,2048]{1,0:T(8,128)(2,1)S(1)}, bf16[88,2048]{1,0:T(8,128)(2,1)S(1)}, u32[]{:S(2)}, u32[]{:S(2)}) collective-permute-start(bf16[88,2048]{1,0:T(8,128)(2,1)S(1)} %get-tuple-element.149), channel_id=1, source_target_pairs={{128,0},{192,64},{256,128},{320,192},{384,256},{448,320},{0,384},{... | collective-permute-start | bytes 1081352 | tf_op jit(solution)/shard_map/cond/branch_0_fun/ppermute | solution.py:199
  187.9 1.9 collective-permute-start.8
  189.8 1.9 collective-permute-start.9
  191.8 23.7 %collective-permute-done.7 = bf16[88,2048]{1,0:T(8,128)(2,1)S(1)} collective-permute-done((bf16[88,2048]{1,0:T(8,128)(2,1)S(1)}, bf16[88,2048]{1,0:T(8,128)(2,1)S(1)}, u32[]{:S(2)}, u32[]{:S(2)}) %collective-permute-start.7) | collective-permute-done | bytes 360480 | tf_op jit(solution)/shard_map/cond/branch_0_fun/ppermute | solution.py:199
  215.5 0.8 fusion
  216.3 6.9 %collective-permute-done.8 = bf16[88,2048]{1,0:T(8,128)(2,1)S(1)} collective-permute-done((bf16[88,2048]{1,0:T(8,128)(2,1)S(1)}, bf16[88,2048]{1,0:T(8,128)(2,1)S(1)}, u32[]{:S(2)}, u32[]{:S(2)}) %collective-permute-start.8) | collective-permute-done | bytes 360480 | tf_op jit(solution)/shard_map/cond/branch_0_fun/ppermute | solution.py:199
  223.2 0.8 fusion.1
  224.1 6.9 %collective-permute-done.9 = bf16[88,2048]{1,0:T(8,128)(2,1)S(1)} collective-permute-done((bf16[88,2048]{1,0:T(8,128)(2,1)S(1)}, bf16[88,2048]{1,0:T(8,128)(2,1)S(1)}, u32[]{:S(2)}, u32[]{:S(2)}) %collective-permute-start.9) | collective-permute-done | bytes 360480 | tf_op jit(solution)/shard_map/cond/branch_0_fun/ppermute | solution.py:199
  230.9 0.8 fusion.2
  (12 shorter events, 0.1 us)
Async XLA Ops:
  2.3 18.9 %collective-permute-start = (bf16[2,128,256]{2,1,0:T(8,128)(2,1)S(1)}, bf16[2,128,256]{2,1,0:T(8,128)(2,1)S(1)}, u32[]{:S(2)}, u32[]{:S(2)}) collective-permute-start(bf16[2,128,256]{2,1,0:T(8,128)(2,1)S(1)} %get-tuple-element.293), channel_id=1, source_target_pairs={{0,4},{4,0},{1,5},{5,1},{2,6},{6,2},{3,7},{7,3},{8,12},{12,8},{9,1... | collective-permute-start | bytes 393224 | tf_op jit(solution)/shard_map/cond/branch_0_fun/ppermute | solution.py:207
  38.5 31.8 %all-to-all-start.1 = ((bf16[4,4,2,2,128,256]{5,4,3,2,1,0:T(8,128)(2,1)}), bf16[4,4,2,2,128,256]{5,4,3,2,1,0:T(8,128)(2,1)}, u32[]{:S(2)}, u32[]{:S(2)}) async-start(bf16[4,4,2,2,128,256]{5,4,3,2,1,0:T(8,128)(2,1)} %broadcast_in_dim.48), calls=%async_computation.1 | async-start | bytes 8388608 | tf_op jit(solution)/shard_map/cond/branch_0_fun/all_to_all | solution.py:219
  43.4 14.4 %collective-permute-start.1 = (bf16[2,128,256]{2,1,0:T(8,128)(2,1)S(1)}, bf16[2,128,256]{2,1,0:T(8,128)(2,1)S(1)}, u32[]{:S(2)}, u32[]{:S(2)}) collective-permute-start(bf16[2,128,256]{2,1,0:T(8,128)(2,1)S(1)} %get-tuple-element.287), channel_id=1, source_target_pairs={{0,4},{4,0},{1,5},{5,1},{2,6},{6,2},{3,7},{7,3},{8,12},{12,8},{9,1... | collective-permute-start | bytes 393224 | tf_op jit(solution)/shard_map/cond/branch_0_fun/ppermute | solution.py:207
  70.3 17.7 %collective-permute-start.2 = (bf16[4,4,2,2,128,256]{5,4,3,2,1,0:T(8,128)(2,1)}, bf16[4,4,2,2,128,256]{5,4,3,2,1,0:T(8,128)(2,1)S(1)}, u32[]{:S(2)}, u32[]{:S(2)}) collective-permute-start(bf16[4,4,2,2,128,256]{5,4,3,2,1,0:T(8,128)(2,1)} %all-to-all-done.1.refs_11_), channel_id=1, source_target_pairs={{0,8},{8,0},{1,9},{9,1},{2,10},{10,2},{3,11},{11,3},{4,12},{12,4},... | collective-permute-start | bytes 12582920 | tf_op jit(solution)/shard_map/cond/branch_0_fun/ppermute | solution.py:223
  88.0 2.0 copy-start
  92.5 56.7 %all-to-all-start.3 = ((bf16[4,4,2,2,128,256]{5,4,3,2,1,0:T(8,128)(2,1)}), bf16[4,4,2,2,128,256]{5,4,3,2,1,0:T(8,128)(2,1)}, u32[]{:S(2)}, u32[]{:S(2)}) async-start(bf16[4,4,2,2,128,256]{5,4,3,2,1,0:T(8,128)(2,1)} %broadcast_in_dim.76), calls=%async_computation.3 | async-start | bytes 8388608 | tf_op jit(solution)/shard_map/cond/branch_0_fun/all_to_all | solution.py:219
  98.4 2.2 copy-start.1
  112.8 0.9 copy-start.18
  113.7 0.9 copy-start.20
  114.6 22.0 %collective-permute-start.3 = (bf16[88,2048]{1,0:T(8,128)(2,1)S(1)}, bf16[88,2048]{1,0:T(8,128)(2,1)S(1)}, u32[]{:S(2)}, u32[]{:S(2)}) collective-permute-start(bf16[88,2048]{1,0:T(8,128)(2,1)S(1)} %get-tuple-element.135.refs_2_), channel_id=1, source_target_pairs={{64,0},{128,64},{192,128},{256,192},{320,256},{384,320},{448,384},... | collective-permute-start | bytes 1081352 | tf_op jit(solution)/shard_map/cond/branch_0_fun/ppermute | solution.py:199
  123.8 16.9 %collective-permute-start.4 = (bf16[88,2048]{1,0:T(8,128)(2,1)S(1)}, bf16[88,2048]{1,0:T(8,128)(2,1)S(1)}, u32[]{:S(2)}, u32[]{:S(2)}) collective-permute-start(bf16[88,2048]{1,0:T(8,128)(2,1)S(1)} %get-tuple-element.136.refs_3_), channel_id=1, source_target_pairs={{64,0},{128,64},{192,128},{256,192},{320,256},{384,320},{448,384},... | collective-permute-start | bytes 1081352 | tf_op jit(solution)/shard_map/cond/branch_0_fun/ppermute | solution.py:199
  133.2 0.7 copy-start.38
  133.9 14.6 %collective-permute-start.5 = (bf16[88,2048]{1,0:T(8,128)(2,1)S(1)}, bf16[88,2048]{1,0:T(8,128)(2,1)S(1)}, u32[]{:S(2)}, u32[]{:S(2)}) collective-permute-start(bf16[88,2048]{1,0:T(8,128)(2,1)S(1)} %get-tuple-element.137.refs_4_), channel_id=1, source_target_pairs={{64,0},{128,64},{192,128},{256,192},{320,256},{384,320},{448,384},... | collective-permute-start | bytes 1081352 | tf_op jit(solution)/shard_map/cond/branch_0_fun/ppermute | solution.py:199
  135.8 0.7 copy-start.40
  136.6 0.7 copy-start.50
  140.8 0.7 copy-start.56
  148.5 0.7 copy-start.62
  149.3 10.6 %collective-permute-start.6 = (bf16[4,4,2,2,128,256]{5,4,3,2,1,0:T(8,128)(2,1)}, bf16[4,4,2,2,128,256]{5,4,3,2,1,0:T(8,128)(2,1)S(1)}, u32[]{:S(2)}, u32[]{:S(2)}) collective-permute-start(bf16[4,4,2,2,128,256]{5,4,3,2,1,0:T(8,128)(2,1)} %all-to-all-done.3.refs_14_), channel_id=1, source_target_pairs={{0,8},{8,0},{1,9},{9,1},{2,10},{10,2},{3,11},{11,3},{4,12},{12,4},... | collective-permute-start | bytes 12582920 | tf_op jit(solution)/shard_map/cond/branch_0_fun/ppermute | solution.py:223
  159.8 1.1 copy-start.19
  161.0 1.1 copy-start.21
  162.1 1.0 copy-start.39
  163.0 1.0 copy-start.41
  164.0 1.0 copy-start.51
  165.0 1.0 copy-start.57
  166.0 1.0 copy-start.63
  179.9 35.6 %collective-permute-start.7 = (bf16[88,2048]{1,0:T(8,128)(2,1)S(1)}, bf16[88,2048]{1,0:T(8,128)(2,1)S(1)}, u32[]{:S(2)}, u32[]{:S(2)}) collective-permute-start(bf16[88,2048]{1,0:T(8,128)(2,1)S(1)} %get-tuple-element.149), channel_id=1, source_target_pairs={{128,0},{192,64},{256,128},{320,192},{384,256},{448,320},{0,384},{... | collective-permute-start | bytes 1081352 | tf_op jit(solution)/shard_map/cond/branch_0_fun/ppermute | solution.py:199
  187.9 35.3 %collective-permute-start.8 = (bf16[88,2048]{1,0:T(8,128)(2,1)S(1)}, bf16[88,2048]{1,0:T(8,128)(2,1)S(1)}, u32[]{:S(2)}, u32[]{:S(2)}) collective-permute-start(bf16[88,2048]{1,0:T(8,128)(2,1)S(1)} %get-tuple-element.150), channel_id=1, source_target_pairs={{128,0},{192,64},{256,128},{320,192},{384,256},{448,320},{0,384},{... | collective-permute-start | bytes 1081352 | tf_op jit(solution)/shard_map/cond/branch_0_fun/ppermute | solution.py:199
  189.8 41.1 %collective-permute-start.9 = (bf16[88,2048]{1,0:T(8,128)(2,1)S(1)}, bf16[88,2048]{1,0:T(8,128)(2,1)S(1)}, u32[]{:S(2)}, u32[]{:S(2)}) collective-permute-start(bf16[88,2048]{1,0:T(8,128)(2,1)S(1)} %get-tuple-element.151), channel_id=1, source_target_pairs={{128,0},{192,64},{256,128},{320,192},{384,256},{448,320},{0,384},{... | collective-permute-start | bytes 1081352 | tf_op jit(solution)/shard_map/cond/branch_0_fun/ppermute | solution.py:199

commit v3 on v2

v3 whole, which is shorter than its diff:
```python
import math

import jax
import jax.numpy as jnp
from jax import lax
from jax.experimental import pallas as pl
from jax.experimental.pallas import tpu as pltpu
from jax.sharding import Mesh, PartitionSpec as P

D = 2048
FF = 5632
STEPS = 2
ROWS = 88
LIMIT = 32
BLK = 256
TOKB = 128
TOK = 1024
NB = D // BLK

rate = 0.2
beta_one = 0.9
beta_two = 0.95
adam_eps = 1e-08
hop_levels = 5
INV_MODEL = 1.0 / math.sqrt(D)
INV_HIDDEN = 1.0 / math.sqrt(FF)


def dot(left, right, right_dim):
    return lax.dot_general(
        left, right, (((1,), (right_dim,)), ((), ())), preferred_element_type=jnp.float32
    )


def pad_rows(value):
    value = value.astype(jnp.float32)
    more = -value.shape[0] % 16
    if more:
        value = jnp.concatenate([value, jnp.zeros((more, value.shape[1]), jnp.float32)], 0)
    return value.astype(jnp.bfloat16)


def step_kernel(step, blended, part, pos, fix, *refs):
    low, rows = part
    pad = -(-rows // 16) * 16
    count = 1 if step else 3
    weights, refs = refs[:count], refs[count:]
    if blended:
        peers, refs = refs[0], refs[1:]
    firsts_in, seconds_in, refs = refs[:count], refs[count : 2 * count], refs[2 * count :]
    mine, theirs, refs = refs[0], refs[1], refs[2:]
    new_w, refs = refs[0], refs[1:]
    if not step:
        m_out, v_out, refs = refs[0], refs[1], refs[2:]
    gu_buf, v_buf, d_buf, h_buf, w_buf, refs = *refs[:5], refs[5:]
    if blended:
        p_buf, refs = refs[0], refs[1:]
    m_buf, s_buf, refs = refs[0], refs[1], refs[2:]
    if not step:
        new_m, new_v, refs = refs[0], refs[1], refs[2:]
    sem, out_sem = refs
    core, high = pos[0], pos[1]

    def block(x, y, z, kind):
        parts = []
        for half, source in enumerate((mine, theirs)):
            from_core = core if half == 0 else 1 - core
            near = jnp.where(from_core == 0, x, y)
            far = jnp.where(from_core == 0, y, x)
            parts.append(source[far, near, jnp.where(high == z, 0, 1), kind])
        return jnp.concatenate(parts, 0)

    def whole(sources, buf, which):
        if step:
            return [pltpu.make_async_copy(sources[0], buf, sem.at[which])]
        return [
            pltpu.make_async_copy(source, buf.at[i], sem.at[which])
            for i, source in enumerate(sources)
        ]

    tensors = whole(weights, w_buf, 0) + (whole([peers], p_buf, 0) if blended else [])
    moments = whole(firsts_in, m_buf, 1) + whole(seconds_in, s_buf, 1)
    for copy in tensors + moments:
        copy.start()
    for copy in tensors:
        copy.wait()

    def load(buf, i, cols):
        value = buf[i, :, cols].astype(jnp.float32)
        return value if step else value[low : low + rows]

    def weight(i, cols):
        mine = load(w_buf, i, cols)
        if blended:
            mine = (mine + load(p_buf, i, cols)) * 0.5
            mine = mine.astype(jnp.bfloat16).astype(jnp.float32)
        return mine

    def prepare(j, _):
        cols = pl.ds(pl.multiple_of(j * BLK, BLK), BLK)
        gu_buf[0:pad, cols] = pad_rows(weight(0, cols))
        gu_buf[pad : 2 * pad, cols] = pad_rows(weight(1, cols))
        v_buf[:, cols] = pad_rows(weight(2, cols))
        return 0

    lax.fori_loop(0, NB, prepare, 0)

    def forward(t, _):
        toks = pl.ds(pl.multiple_of(t * 256, 256), 256)
        gu = jnp.zeros((2 * pad, 256), jnp.float32)
        back = jnp.zeros((pad, 256), jnp.float32)
        for j in range(NB):
            cols = slice(j * BLK, (j + 1) * BLK)
            gu += dot(gu_buf[:, cols], block(t, j % 4, j // 4, 0), 1)
        for j in range(NB):
            cols = slice(j * BLK, (j + 1) * BLK)
            back += dot(v_buf[:, cols], block(t, j % 4, j // 4, 1), 1)
        gate, upper = gu[:pad] * INV_MODEL, gu[pad:] * INV_MODEL
        back = back * INV_HIDDEN
        sigma = jax.nn.sigmoid(gate)
        gs = gate * sigma
        h_buf[:, toks] = (gs * upper).astype(jnp.bfloat16)
        d_gate = back * upper * sigma * (1.0 + gate * (1.0 - sigma))
        d_buf[0:pad, toks] = d_gate.astype(jnp.bfloat16)
        d_buf[pad : 2 * pad, toks] = (back * gs).astype(jnp.bfloat16)
        return 0

    lax.fori_loop(0, TOK // 256, forward, 0)
    rate_one, inv_two = fix[0], fix[1]
    for copy in moments:
        copy.wait()

    def backward(j, _):
        cols = pl.ds(pl.multiple_of(j * BLK, BLK), BLK)
        y, z = j % 4, j // 4
        gu = jnp.zeros((2 * pad, BLK), jnp.float32)
        down = jnp.zeros((pad, BLK), jnp.float32)
        for x in range(4):
            toks = slice(x * 256, (x + 1) * 256)
            gu += dot(d_buf[:, toks], block(x, y, z, 0), 0)
            down += dot(h_buf[:, toks], block(x, y, z, 1), 0)
        grads = (gu[:rows], gu[pad : pad + rows], down[:rows])
        for i, grad in enumerate(grads):
            grad = grad * (INV_HIDDEN if i == 2 else INV_MODEL)
            first = beta_one * load(m_buf, i, cols) + (1.0 - beta_one) * grad
            second = beta_two * load(s_buf, i, cols) + (1.0 - beta_two) * grad * grad
            change = (first * rate_one) / (jnp.sqrt(second * inv_two) + adam_eps)
            new_w[i, :, cols] = (weight(i, cols) - change).astype(jnp.bfloat16)
            if not step:
                new_m[i, :, cols] = first
                new_v[i, :, cols] = second
                for buf, out in ((new_m, m_out), (new_v, v_out)):
                    pltpu.make_async_copy(
                        buf.at[i, :, cols], out.at[i, :, cols], out_sem
                    ).start()
        return 0

    lax.fori_loop(0, NB, backward, 0)
    if not step:
        for buf, out in ((new_m, m_out), (new_v, v_out)):
            pltpu.make_async_copy(buf, out, out_sem).wait()


def run_step(step, part, pos, fix, weights, peers, firsts, seconds, gathered):
    smem = pl.BlockSpec(memory_space=pltpu.SMEM)
    vmem = pl.BlockSpec(memory_space=pltpu.VMEM)
    hbm = pl.BlockSpec(memory_space=pltpu.HBM)
    blended = peers is not None
    rows = part[1]
    pad = -(-rows // 16) * 16
    args = [*weights, *([peers] if blended else []), *firsts, *seconds, *gathered]
    trio = (3, rows, D)
    held = trio if step else (3, ROWS, D)
    outs = [jax.ShapeDtypeStruct(trio, jnp.bfloat16)]
    if not step:
        outs += [jax.ShapeDtypeStruct(trio, jnp.float32)] * 2
    mults = 6 * rows * TOK * D

    def body(*refs):
        step_kernel(step, blended, part, *refs)

    return pl.pallas_call(
        body,
        out_shape=outs,
        in_specs=[smem, smem] + [hbm] * (len(args) - 2) + [vmem] * 2,
        out_specs=[vmem] + [hbm] * (len(outs) - 1),
        scratch_shapes=[
            pltpu.VMEM((2 * pad, D), jnp.bfloat16),
            pltpu.VMEM((pad, D), jnp.bfloat16),
            pltpu.VMEM((2 * pad, TOK), jnp.bfloat16),
            pltpu.VMEM((pad, TOK), jnp.bfloat16),
            pltpu.VMEM(held, jnp.bfloat16),
        ]
        + ([pltpu.VMEM(held, jnp.bfloat16)] if blended else [])
        + [pltpu.VMEM(held, firsts[0].dtype)] * 2
        + ([] if step else [pltpu.VMEM(trio, jnp.float32)] * 2)
        + [pltpu.SemaphoreType.DMA((2,)), pltpu.SemaphoreType.DMA],
        compiler_params=pltpu.CompilerParams(vmem_limit_bytes=LIMIT * 2**20),
        cost_estimate=pl.CostEstimate(
            flops=2 * mults, bytes_accessed=16 * 2**20, transcendentals=rows * TOK
        ),
        name="adam_step",
    )(pos, fix, *args)


def shift_rep(value, hops):
    return lax.ppermute(value, "zl", [((i + hops) % 8, i) for i in range(8)])


def blend(mine, peer):
    return ((mine.astype(jnp.float32) + peer.astype(jnp.float32)) * 0.5).astype(jnp.bfloat16)


def z_partner(value):
    return lax.ppermute(value, "zh", [(0, 1), (1, 0)])


def ring_gather(value, x_core):
    groups = []
    for core in range(2):
        for k in range(4):
            if core == x_core:
                groups.append([i * 8 + core * 4 + k for i in range(4)])
            else:
                groups.append([k * 8 + core * 4 + i for i in range(4)])
    copies = jnp.broadcast_to(value[None], (4,) + value.shape)
    return lax.all_to_all(copies, ("x", "c", "y"), 0, 0, axis_index_groups=groups)


def core_swap(value):
    return lax.ppermute(value, "c", [(0, 1), (1, 0)])


def corrections(steps_done, step):
    count = (steps_done[0] + step + 1).astype(jnp.float32)
    fix_one = 1.0 - jnp.power(jnp.float32(beta_one), count)
    fix_two = 1.0 - jnp.power(jnp.float32(beta_two), count)
    return jnp.stack([rate / fix_one, 1.0 / fix_two])


def both_steps(power, steps_done, *arrays):
    hops = [2 ** ((power + s) % hop_levels) % 8 for s in range(STEPS)]
    weights = [a[0] for a in arrays[0:3]]
    firsts = [a[0] for a in arrays[3:6]]
    seconds = [a[0] for a in arrays[6:9]]
    inputs, cotangent = arrays[9:]
    pos = jnp.stack([lax.axis_index("c"), lax.axis_index("zh")]).astype(jnp.int32)
    own = [jnp.stack([inputs[s], cotangent[s]]) for s in range(STEPS)]
    other = [z_partner(v) for v in own]
    mine = ring_gather(ring_gather(jnp.stack((own[0], other[0])), 0), 1)
    mine, other[1] = lax.optimization_barrier((mine, other[1]))
    theirs = core_swap(mine)
    part_one = ring_gather(jnp.stack((own[1], other[1])), 0)
    theirs, part_one = lax.optimization_barrier((theirs, part_one))
    parts = [(0, 48), (48, 40)] if any(hops) else [(0, ROWS)]
    fix = corrections(steps_done, 0)
    after = [
        run_step(0, part, pos, fix, weights, None, firsts, seconds, (mine, theirs))
        for part in parts
    ]
    mine = ring_gather(part_one, 1)
    peers = [None] * len(parts)
    if hops[0]:
        peers = [shift_rep(a[0], hops[0]) for a in after]
        peers[0], _ = lax.optimization_barrier((peers[0], after[-1][0]))
        mine, peers[0] = lax.optimization_barrier((mine, peers[0]))
    else:
        mine, after = lax.optimization_barrier((mine, after))
    theirs = core_swap(mine)
    fix = corrections(steps_done, 1)
    new = []
    for part, peer, (w, m, v) in zip(parts, peers, after):
        if new and hops[0]:
            peer, _ = lax.optimization_barrier((peer, new[-1]))
        new += run_step(1, part, pos, fix, [w], peer, [m], [v], (mine, theirs))
    if hops[1]:
        sent = list(new)
        if hops[0]:
            sent[0], _ = lax.optimization_barrier((new[0], peers[1]))
        others = [shift_rep(w, hops[1]) for w in sent]
        others[0], _ = lax.optimization_barrier((others[0], new[1]))
        first = blend(new[0], others[0])
        first, others[1] = lax.optimization_barrier((first, others[1]))
        new = [first, blend(new[1], others[1])]
    return tuple(jnp.concatenate([w[i] for w in new], 0)[None] for i in range(3))


def local(steps_done, *arrays):
    branches = [
        lambda *operands, power=p: both_steps(power, *operands) for p in range(hop_levels)
    ]
    return lax.switch(steps_done[0] % hop_levels, branches, steps_done, *arrays)


def solution(mesh):
    fine = Mesh(mesh.devices.reshape(8, 4, 2, 2, 4), ("zl", "x", "c", "zh", "y"))
    rep, tp = ("zl", "x", "c"), ("zh", "y")
    weight = P(rep, tp, None)
    return jax.shard_map(
        local,
        mesh=fine,
        in_specs=(P(),) + (weight,) * 9 + (P(None, rep, tp),) * 2,
        out_specs=(weight,) * 3,
        check_vma=False,
    )
```

time: 235 us -> 187 us (0.80); the launches traced: 232 us -> 187 us
  waiting for transfers between devices: 71.6 us -> 33.3 us
  Pallas kernels: 25.2 us -> 39.8 us
  starting transfers between devices: 79.3 us -> 65.9 us
  local copies, waits for them, and re-layouts: 23 us -> 14.3 us
    ppermute x6 -> x2, waiting for transfers between devices: 47.9 us -> 9.68 us  [shift_rep(): return lax.ppermute(value, 'zl', [((i + hops) % 8, i) for i in range(8)])]
    pallas_call x2 -> x4, Pallas kernels: 25.2 us -> 39.8 us  [run_step(): pl.pallas_call(body, out_shape=outs, in_specs=[smem, smem] + [hbm] * (len...]
    ppermute x6 -> x2, starting transfers between devices: 32.4 us -> 18.6 us  [shift_rep(): return lax.ppermute(value, 'zl', [((i + hops) % 8, i) for i in range(8)])]
    cond x32 -> x48, local copies, waits for them, and re-layouts: 16.7 us -> 7.9 us
  transfers between devices with their start and end apart: 12 -> 8, of which waited for: 9 -> 5; matrix products, arithmetic and copies ran while one was open for 1% -> 0% of each run, Pallas kernels for 5% -> 16%
where the time goes in v3:
time: 187 us
  starting transfers between devices  65.9 us (35%)
  Pallas kernels  39.8 us (21%)
  waiting for transfers between devices  33.3 us (18%)
  blocking collectives  26.8 us (14%)
  local copies, waits for them, and re-layouts  14.3 us (8%)
  other arithmetic  2.93 us (2%)
  loops' own time  2.27 us (1%)
    pallas_call x4, Pallas kernels, run_step(): pl.pallas_call(body, out_shape=outs, in_specs=[smem, smem] + [hbm] * (len...  39.8 us
    ppermute x2, starting transfers between devices, z_partner(): return lax.ppermute(value, 'zh', [(0, 1), (1, 0)])  28.3 us
    all_to_all x2, blocking collectives, ring_gather(): lax.all_to_all(copies, ('x', 'c', 'y'), 0, 0, axis_index_groups=groups)  26.8 us
    ppermute x2, starting transfers between devices, shift_rep(): return lax.ppermute(value, 'zl', [((i + hops) % 8, i) for i in range(8)])  18.6 us
    all_to_all x2, waiting for transfers between devices, ring_gather(): lax.all_to_all(copies, ('x', 'c', 'y'), 0, 0, axis_index_groups=groups)  12.5 us
    all_to_all x2, starting transfers between devices, ring_gather(): lax.all_to_all(copies, ('x', 'c', 'y'), 0, 0, axis_index_groups=groups)  9.82 us
    ppermute x2, waiting for transfers between devices, shift_rep(): return lax.ppermute(value, 'zl', [((i + hops) % 8, i) for i in range(8)])  9.68 us
    ppermute x2, starting transfers between devices, core_swap(): return lax.ppermute(value, 'c', [(0, 1), (1, 0)])  9.25 us
  transfers between devices with their start and end apart: 8, of which 5 were waited for; matrix products, arithmetic and copies ran while one was open for 0% of the time, Pallas kernels for 16%

profile of v3, /device:TPU:1, one launch (start us, length us, event | category | flops | bytes accessed | tf_op | source)
XLA Modules:
  0.0 186.7 jit_solution(11169468128031950340)
XLA Ops:
  1.3 185.4 %conditional.1 = (bf16[1,88,2048]{2,1,0:T(8,128)(2,1)}, bf16[1,88,2048]{2,1,0:T(8,128)(2,1)}, bf16[1,88,2048]{2,1,0:T(8,128)(2,1)}) conditional(s32[]{:T(128)} %clamp.3, (s32[1]{0:T(128)}, bf16[1,88,2048]{2,1,0:T(8,128)(2,1)}, bf16[1,88,2048]{2,1,0:T(8,128)(2,1)}, bf16[1,88,2048]{2,1,0:T(8,128)(2,1)}, ...), branch_computations={%region_0.1_spmd, %region_1.2_spmd, %region_2.3_spmd, %region_3.4_... | conditional | flops 4434444288 | bytes 233407776 | solution.py:292
  1.6 1.0 fusion.19
  2.5 16.3 %collective-permute-start.26 = (bf16[2,128,256]{2,1,0:T(8,128)(2,1)S(1)}, bf16[2,128,256]{2,1,0:T(8,128)(2,1)S(1)}, u32[]{:S(2)}, u32[]{:S(2)}) collective-permute-start(bf16[2,128,256]{2,1,0:T(8,128)(2,1)S(1)} %get-tuple-element.341), channel_id=1, source_target_pairs={{0,4},{4,0},{1,5},{5,1},{2,6},{6,2},{3,7},{7,3},{8,12},{12,8},{9,1... | collective-permute-start | bytes 393224 | tf_op jit(solution)/shard_map/cond/branch_4_fun/ppermute | solution.py:215
  18.8 2.6 %collective-permute-done.26 = bf16[2,128,256]{2,1,0:T(8,128)(2,1)S(1)} collective-permute-done((bf16[2,128,256]{2,1,0:T(8,128)(2,1)S(1)}, bf16[2,128,256]{2,1,0:T(8,128)(2,1)S(1)}, u32[]{:S(2)}, u32[]{:S(2)}) %collective-permute-start.26) | collective-permute-done | bytes 131104 | tf_op jit(solution)/shard_map/cond/branch_4_fun/ppermute | solution.py:215
  21.5 0.1 broadcast_in_dim.114
  21.6 14.6 %all_to_all.88 = bf16[4,2,2,128,256]{4,3,2,1,0:T(8,128)(2,1)S(1)} all-to-all(bf16[4,2,2,128,256]{4,3,2,1,0:T(8,128)(2,1)S(1)} %broadcast_in_dim.114), channel_id=1, replica_groups={{0,16,32,48},{1,17,33,49},{2,18,34,50},{3,19,35,51},{8,9,10,11},{24,25,..., dimensions={0} | all-to-all | bytes 2097152 | tf_op jit(solution)/shard_map/cond/branch_4_fun/all_to_all | solution.py:227
  36.2 2.6 %broadcast_in_dim.115 = bf16[4,4,2,2,128,256]{5,4,3,2,1,0:T(8,128)(2,1)} broadcast(bf16[4,2,2,128,256]{4,3,2,1,0:T(8,128)(2,1)S(1)} %all_to_all.88), dimensions={1,2,3,4,5} | broadcast | bytes 5242880 | tf_op jit(solution)/shard_map/cond/branch_4_fun/broadcast_in_dim | solution.py:226
  38.8 4.8 %all-to-all-start.17 = ((bf16[4,4,2,2,128,256]{5,4,3,2,1,0:T(8,128)(2,1)}), bf16[4,4,2,2,128,256]{5,4,3,2,1,0:T(8,128)(2,1)}, u32[]{:S(2)}, u32[]{:S(2)}) async-start(bf16[4,4,2,2,128,256]{5,4,3,2,1,0:T(8,128)(2,1)} %broadcast_in_dim.115), calls=%async_computation.17 | async-start | bytes 8388608 | tf_op jit(solution)/shard_map/cond/branch_4_fun/all_to_all | solution.py:227
  43.6 12.0 %collective-permute-start.27 = (bf16[2,128,256]{2,1,0:T(8,128)(2,1)S(1)}, bf16[2,128,256]{2,1,0:T(8,128)(2,1)S(1)}, u32[]{:S(2)}, u32[]{:S(2)}) collective-permute-start(bf16[2,128,256]{2,1,0:T(8,128)(2,1)S(1)} %get-tuple-element.335), channel_id=1, source_target_pairs={{0,4},{4,0},{1,5},{5,1},{2,6},{6,2},{3,7},{7,3},{8,12},{12,8},{9,1... | collective-permute-start | bytes 393224 | tf_op jit(solution)/shard_map/cond/branch_4_fun/ppermute | solution.py:215
  55.7 2.4 %collective-permute-done.27 = bf16[2,128,256]{2,1,0:T(8,128)(2,1)S(1)} collective-permute-done((bf16[2,128,256]{2,1,0:T(8,128)(2,1)S(1)}, bf16[2,128,256]{2,1,0:T(8,128)(2,1)S(1)}, u32[]{:S(2)}, u32[]{:S(2)}) %collective-permute-start.27) | collective-permute-done | bytes 131104 | tf_op jit(solution)/shard_map/cond/branch_4_fun/ppermute | solution.py:215
  58.1 12.5 %all-to-all-done.17.refs_11_ = bf16[4,4,2,2,128,256]{5,4,3,2,1,0:T(8,128)(2,1)} async-done(((bf16[4,4,2,2,128,256]{5,4,3,2,1,0:T(8,128)(2,1)}), bf16[4,4,2,2,128,256]{5,4,3,2,1,0:T(8,128)(2,1)}, u32[]{:S(2)}, u32[]{:S(2)}) %all-to-all-start.17) | async-done | bytes 4194336 | tf_op jit(solution)/shard_map/cond/branch_4_fun/all_to_all | solution.py:227
  70.6 5.6 %collective-permute-start.28 = (bf16[4,4,2,2,128,256]{5,4,3,2,1,0:T(8,128)(2,1)}, bf16[4,4,2,2,128,256]{5,4,3,2,1,0:T(8,128)(2,1)S(1)}, u32[]{:S(2)}, u32[]{:S(2)}) collective-permute-start(bf16[4,4,2,2,128,256]{5,4,3,2,1,0:T(8,128)(2,1)} %all-to-all-done.17.refs_11_), channel_id=1, source_target_pairs={{0,8},{8,0},{1,9},{9,1},{2,10},{10,2},{3,11},{11,3},{4,12},{12,4},... | collective-permute-start | bytes 12582920 | tf_op jit(solution)/shard_map/cond/branch_4_fun/ppermute | solution.py:231
  76.2 0.1 broadcast_in_dim.116
  76.3 12.2 %all_to_all.89 = bf16[4,2,2,128,256]{4,3,2,1,0:T(8,128)(2,1)S(1)} all-to-all(bf16[4,2,2,128,256]{4,3,2,1,0:T(8,128)(2,1)S(1)} %broadcast_in_dim.116), channel_id=1, replica_groups={{0,16,32,48},{1,17,33,49},{2,18,34,50},{3,19,35,51},{8,9,10,11},{24,25,..., dimensions={0} | all-to-all | bytes 2097152 | tf_op jit(solution)/shard_map/cond/branch_4_fun/all_to_all | solution.py:227
  88.5 0.0 collective-permute-done.28.refs_12_
  88.5 2.0 %copy-done.6 = bf16[4,4,2,2,128,256]{5,4,3,2,1,0:T(8,128)(2,1)} copy-done((bf16[4,4,2,2,128,256]{5,4,3,2,1,0:T(8,128)(2,1)}, bf16[4,4,2,2,128,256]{5,4,3,2,1,0:T(8,128)(2,1)S(1)}, u32[]{:S(2)}) %copy-start.6) | copy-done | bytes 4194328 | tf_op jit(solution)/shard_map/cond
  90.5 2.6 %broadcast_in_dim.117 = bf16[4,4,2,2,128,256]{5,4,3,2,1,0:T(8,128)(2,1)} broadcast(bf16[4,2,2,128,256]{4,3,2,1,0:T(8,128)(2,1)S(1)} %all_to_all.89), dimensions={1,2,3,4,5} | broadcast | bytes 5242880 | tf_op jit(solution)/shard_map/cond/branch_4_fun/broadcast_in_dim | solution.py:226
  93.1 0.0 copy-start.71
  93.1 0.0 copy-start.76
  93.1 0.0 copy-start.81
  93.1 5.0 %all-to-all-start.19 = ((bf16[4,4,2,2,128,256]{5,4,3,2,1,0:T(8,128)(2,1)}), bf16[4,4,2,2,128,256]{5,4,3,2,1,0:T(8,128)(2,1)}, u32[]{:S(2)}, u32[]{:S(2)}) async-start(bf16[4,4,2,2,128,256]{5,4,3,2,1,0:T(8,128)(2,1)} %broadcast_in_dim.117), calls=%async_computation.19 | async-start | bytes 8388608 | tf_op jit(solution)/shard_map/cond/branch_4_fun/all_to_all | solution.py:227
  98.9 0.1 pad_maximum_fusion.29.refs_1_
  99.0 0.1 pad_add_fusion.4.refs_0_
  99.1 0.0 copy-done.48
  99.1 0.0 copy-done.56
  99.1 0.0 copy-done.61
  99.1 0.0 copy-done.66
  99.1 0.0 copy-done.71
  99.1 0.0 copy-done.76
  99.1 0.0 copy-done.81
  99.1 0.0 copy-start.7
  99.1 2.2 %copy-done.7 = bf16[4,4,2,2,128,256]{5,4,3,2,1,0:T(8,128)(2,1)S(1)} copy-done((bf16[4,4,2,2,128,256]{5,4,3,2,1,0:T(8,128)(2,1)S(1)}, bf16[4,4,2,2,128,256]{5,4,3,2,1,0:T(8,128)(2,1)}, u32[]{:S(2)}) %copy-start.7) | copy-done | bytes 4194328 | tf_op jit(solution)/shard_map/cond
  101.3 0.0 copy-start.72
  101.3 0.0 copy-start.77
  101.3 0.0 copy-start.82
  101.4 0.0 copy-start.86
  101.4 0.0 copy-start.90
  101.4 10.4 %adam_step.33 = (bf16[3,40,2048]{2,1,0:T(8,128)(2,1)S(1)}, f32[3,40,2048]{2,1,0:T(8,128)S(1)}, f32[3,40,2048]{2,1,0:T(8,128)S(1)}) custom-call(s32[2]{0:T(128)S(1)} %pad_add_fusion.4.refs_0_, f32[2]{0:T(128)S(1)} %pad_maximum_fusion.29.refs_1_, bf16[88,2048]{1,0:T(8,128)(2,1)S(1)} %bitcast.165, bf16[88,2048]{1,0:T(8,128)(2,1)S(1)} %bitcast.174, ...), custom_call_target="tpu_custom_call" | custom-call | flops 1006632960 | bytes 16777216 | tf_op jit(solution)/shard_map/cond/branch_4_fun/adam_step/pallas_call | solution.py:182
  111.8 0.0 copy-start.18
  111.8 1.0 copy-done.18
  112.8 0.8 copy-done.40
  113.6 0.0 copy-done.49
  113.6 0.0 copy-done.57
  113.6 0.0 copy-done.62
  113.6 0.0 copy-done.67
  113.6 0.0 copy-done.72
  113.6 10.7 %adam_step.32 = (bf16[3,48,2048]{2,1,0:T(8,128)(2,1)S(1)}, f32[3,48,2048]{2,1,0:T(8,128)S(1)}, f32[3,48,2048]{2,1,0:T(8,128)S(1)}) custom-call(s32[2]{0:T(128)S(1)} %pad_add_fusion.4.refs_0_, f32[2]{0:T(128)S(1)} %pad_maximum_fusion.29.refs_1_, bf16[88,2048]{1,0:T(8,128)(2,1)S(1)} %bitcast.166, bf16[88,2048]{1,0:T(8,128)(2,1)S(1)} %bitcast.175, ...), custom_call_target="tpu_custom_call" | custom-call | flops 1207959552 | bytes 16777216 | tf_op jit(solution)/shard_map/cond/branch_4_fun/adam_step/pallas_call | solution.py:182
  124.4 0.8 copy-done.32
  125.2 0.0 all-to-all-done.19.refs_5_
  125.2 3.7 %collective-permute-start.29 = (bf16[4,4,2,2,128,256]{5,4,3,2,1,0:T(8,128)(2,1)}, bf16[4,4,2,2,128,256]{5,4,3,2,1,0:T(8,128)(2,1)S(1)}, u32[]{:S(2)}, u32[]{:S(2)}) collective-permute-start(bf16[4,4,2,2,128,256]{5,4,3,2,1,0:T(8,128)(2,1)} %all-to-all-done.19.refs_5_), channel_id=1, source_target_pairs={{0,8},{8,0},{1,9},{9,1},{2,10},{10,2},{3,11},{11,3},{4,12},{12,4},... | collective-permute-start | bytes 12582920 | tf_op jit(solution)/shard_map/cond/branch_4_fun/ppermute | solution.py:231
  129.7 0.1 pad_maximum_fusion.28.refs_1_
  129.8 6.1 %collective-permute-done.29.refs_6_ = bf16[4,4,2,2,128,256]{5,4,3,2,1,0:T(8,128)(2,1)S(1)} collective-permute-done((bf16[4,4,2,2,128,256]{5,4,3,2,1,0:T(8,128)(2,1)}, bf16[4,4,2,2,128,256]{5,4,3,2,1,0:T(8,128)(2,1)S(1)}, u32[]{:S(2)}, u32[]{:S(2)}) %collective-permute-start.29) | collective-permute-done | bytes 4194336 | tf_op jit(solution)/shard_map/cond/branch_4_fun/ppermute | solution.py:231
  135.9 1.1 copy-done.33
  137.0 9.3 %adam_step.34 = bf16[3,48,2048]{2,1,0:T(8,128)(2,1)S(1)} custom-call(s32[2]{0:T(128)S(1)} %pad_add_fusion.4.refs_0_, f32[2]{0:T(128)S(1)} %pad_maximum_fusion.28.refs_1_, bf16[3,48,2048]{2,1,0:T(8,128)(2,1)S(1)} %copy-done.33, f32[3,48,2048]{2,1,0:T(8,128)S(1)} %get-tuple-element.252.refs_3_, f32[3,48,2048]{2,1,0:T(8,128)S(1)} %get-tuple-element.253.refs_4_, ...), custom_call_target="tpu_custom_call" | custom-call | flops 1207959552 | bytes 16777216 | tf_op jit(solution)/shard_map/cond/branch_4_fun/adam_step/pallas_call | solution.py:182
  146.2 9.3 %collective-permute-start.30 = (bf16[3,48,2048]{2,1,0:T(8,128)(2,1)S(1)}, bf16[3,48,2048]{2,1,0:T(8,128)(2,1)S(1)}, u32[]{:S(2)}, u32[]{:S(2)}) collective-permute-start(bf16[3,48,2048]{2,1,0:T(8,128)(2,1)S(1)} %adam_step.34), channel_id=1, source_target_pairs={{64,0},{128,64},{192,128},{256,192},{320,256},{384,320},{448,384},... | collective-permute-start | bytes 1769480 | tf_op jit(solution)/shard_map/cond/branch_4_fun/ppermute | solution.py:207
  155.6 9.4 %adam_step.35 = bf16[3,40,2048]{2,1,0:T(8,128)(2,1)S(1)} custom-call(s32[2]{0:T(128)S(1)} %pad_add_fusion.4.refs_0_, f32[2]{0:T(128)S(1)} %pad_maximum_fusion.28.refs_1_, bf16[3,40,2048]{2,1,0:T(8,128)(2,1)S(1)} %copy-done.41, f32[3,40,2048]{2,1,0:T(8,128)S(1)} %get-tuple-element.256.refs_3_, f32[3,40,2048]{2,1,0:T(8,128)S(1)} %copy-done.19, ...), custom_call_target="tpu_custom_call" | custom-call | flops 1006632960 | bytes 16777216 | tf_op jit(solution)/shard_map/cond/branch_4_fun/adam_step/pallas_call | solution.py:182
  165.0 9.3 %collective-permute-start.31 = (bf16[3,40,2048]{2,1,0:T(8,128)(2,1)S(1)}, bf16[3,40,2048]{2,1,0:T(8,128)(2,1)S(1)}, u32[]{:S(2)}, u32[]{:S(2)}) collective-permute-start(bf16[3,40,2048]{2,1,0:T(8,128)(2,1)S(1)} %adam_step.35), channel_id=1, source_target_pairs={{64,0},{128,64},{192,128},{256,192},{320,256},{384,320},{448,384},... | collective-permute-start | bytes 1474568 | tf_op jit(solution)/shard_map/cond/branch_4_fun/ppermute | solution.py:207
  174.3 0.0 collective-permute-done.30
  174.3 0.2 multiply_convert_fusion.4
  174.5 9.7 %collective-permute-done.31 = bf16[3,40,2048]{2,1,0:T(8,128)(2,1)S(1)} collective-permute-done((bf16[3,40,2048]{2,1,0:T(8,128)(2,1)S(1)}, bf16[3,40,2048]{2,1,0:T(8,128)(2,1)S(1)}, u32[]{:S(2)}, u32[]{:S(2)}) %collective-permute-start.31) | collective-permute-done | bytes 491552 | tf_op jit(solution)/shard_map/cond/branch_4_fun/ppermute | solution.py:207
  184.2 0.1 multiply_convert_fusion.5
  184.4 0.8 maximum_bitcast_fusion.11
  185.2 0.8 maximum_bitcast_fusion.10
  185.9 0.8 maximum_bitcast_fusion.9
  (26 shorter events, 0.2 us)
Async XLA Ops:
  2.5 18.9 %collective-permute-start.26 = (bf16[2,128,256]{2,1,0:T(8,128)(2,1)S(1)}, bf16[2,128,256]{2,1,0:T(8,128)(2,1)S(1)}, u32[]{:S(2)}, u32[]{:S(2)}) collective-permute-start(bf16[2,128,256]{2,1,0:T(8,128)(2,1)S(1)} %get-tuple-element.341), channel_id=1, source_target_pairs={{0,4},{4,0},{1,5},{5,1},{2,6},{6,2},{3,7},{7,3},{8,12},{12,8},{9,1... | collective-permute-start | bytes 393224 | tf_op jit(solution)/shard_map/cond/branch_4_fun/ppermute | solution.py:215
  38.8 31.8 %all-to-all-start.17 = ((bf16[4,4,2,2,128,256]{5,4,3,2,1,0:T(8,128)(2,1)}), bf16[4,4,2,2,128,256]{5,4,3,2,1,0:T(8,128)(2,1)}, u32[]{:S(2)}, u32[]{:S(2)}) async-start(bf16[4,4,2,2,128,256]{5,4,3,2,1,0:T(8,128)(2,1)} %broadcast_in_dim.115), calls=%async_computation.17 | async-start | bytes 8388608 | tf_op jit(solution)/shard_map/cond/branch_4_fun/all_to_all | solution.py:227
  43.6 14.4 %collective-permute-start.27 = (bf16[2,128,256]{2,1,0:T(8,128)(2,1)S(1)}, bf16[2,128,256]{2,1,0:T(8,128)(2,1)S(1)}, u32[]{:S(2)}, u32[]{:S(2)}) collective-permute-start(bf16[2,128,256]{2,1,0:T(8,128)(2,1)S(1)} %get-tuple-element.335), channel_id=1, source_target_pairs={{0,4},{4,0},{1,5},{5,1},{2,6},{6,2},{3,7},{7,3},{8,12},{12,8},{9,1... | collective-permute-start | bytes 393224 | tf_op jit(solution)/shard_map/cond/branch_4_fun/ppermute | solution.py:215
  70.6 17.9 %collective-permute-start.28 = (bf16[4,4,2,2,128,256]{5,4,3,2,1,0:T(8,128)(2,1)}, bf16[4,4,2,2,128,256]{5,4,3,2,1,0:T(8,128)(2,1)S(1)}, u32[]{:S(2)}, u32[]{:S(2)}) collective-permute-start(bf16[4,4,2,2,128,256]{5,4,3,2,1,0:T(8,128)(2,1)} %all-to-all-done.17.refs_11_), channel_id=1, source_target_pairs={{0,8},{8,0},{1,9},{9,1},{2,10},{10,2},{3,11},{11,3},{4,12},{12,4},... | collective-permute-start | bytes 12582920 | tf_op jit(solution)/shard_map/cond/branch_4_fun/ppermute | solution.py:231
  88.5 2.0 %copy-start.6 = (bf16[4,4,2,2,128,256]{5,4,3,2,1,0:T(8,128)(2,1)}, bf16[4,4,2,2,128,256]{5,4,3,2,1,0:T(8,128)(2,1)S(1)}, u32[]{:S(2)}) copy-start(bf16[4,4,2,2,128,256]{5,4,3,2,1,0:T(8,128)(2,1)S(1)} %collective-permute-done.28.refs_12_) | copy-start | bytes 12582916 | tf_op jit(solution)/shard_map/cond
  93.1 6.0 %copy-start.48 = (bf16[1,88,2048]{2,1,0:T(8,128)(2,1)S(1)}, bf16[1,88,2048]{2,1,0:T(8,128)(2,1)}, u32[]{:S(2)}) copy-start(bf16[1,88,2048]{2,1,0:T(8,128)(2,1)} %get-tuple-element.235) | copy-start | bytes 1081348 | tf_op jit(solution)/shard_map/cond
  93.1 6.0 %copy-start.56 = (bf16[1,88,2048]{2,1,0:T(8,128)(2,1)S(1)}, bf16[1,88,2048]{2,1,0:T(8,128)(2,1)}, u32[]{:S(2)}) copy-start(bf16[1,88,2048]{2,1,0:T(8,128)(2,1)} %get-tuple-element.236) | copy-start | bytes 1081348 | tf_op jit(solution)/shard_map/cond
  93.1 6.0 %copy-start.61 = (bf16[1,88,2048]{2,1,0:T(8,128)(2,1)S(1)}, bf16[1,88,2048]{2,1,0:T(8,128)(2,1)}, u32[]{:S(2)}) copy-start(bf16[1,88,2048]{2,1,0:T(8,128)(2,1)} %get-tuple-element.237) | copy-start | bytes 1081348 | tf_op jit(solution)/shard_map/cond
  93.1 6.0 %copy-start.66 = (bf16[1,88,2048]{2,1,0:T(8,128)(2,1)S(1)}, bf16[1,88,2048]{2,1,0:T(8,128)(2,1)}, u32[]{:S(2)}) copy-start(bf16[1,88,2048]{2,1,0:T(8,128)(2,1)} %get-tuple-element.238) | copy-start | bytes 1081348 | tf_op jit(solution)/shard_map/cond
  93.1 6.0 %copy-start.71 = (bf16[1,88,2048]{2,1,0:T(8,128)(2,1)S(1)}, bf16[1,88,2048]{2,1,0:T(8,128)(2,1)}, u32[]{:S(2)}) copy-start(bf16[1,88,2048]{2,1,0:T(8,128)(2,1)} %get-tuple-element.239) | copy-start | bytes 1081348 | tf_op jit(solution)/shard_map/cond
  93.1 6.0 %copy-start.76 = (bf16[1,88,2048]{2,1,0:T(8,128)(2,1)S(1)}, bf16[1,88,2048]{2,1,0:T(8,128)(2,1)}, u32[]{:S(2)}) copy-start(bf16[1,88,2048]{2,1,0:T(8,128)(2,1)} %get-tuple-element.240) | copy-start | bytes 1081348 | tf_op jit(solution)/shard_map/cond
  93.1 6.0 %copy-start.81 = (bf16[1,88,2048]{2,1,0:T(8,128)(2,1)S(1)}, bf16[1,88,2048]{2,1,0:T(8,128)(2,1)}, u32[]{:S(2)}) copy-start(bf16[1,88,2048]{2,1,0:T(8,128)(2,1)} %get-tuple-element.241) | copy-start | bytes 1081348 | tf_op jit(solution)/shard_map/cond
  93.1 32.1 %all-to-all-start.19 = ((bf16[4,4,2,2,128,256]{5,4,3,2,1,0:T(8,128)(2,1)}), bf16[4,4,2,2,128,256]{5,4,3,2,1,0:T(8,128)(2,1)}, u32[]{:S(2)}, u32[]{:S(2)}) async-start(bf16[4,4,2,2,128,256]{5,4,3,2,1,0:T(8,128)(2,1)} %broadcast_in_dim.117), calls=%async_computation.19 | async-start | bytes 8388608 | tf_op jit(solution)/shard_map/cond/branch_4_fun/all_to_all | solution.py:227
  99.1 2.2 %copy-start.7 = (bf16[4,4,2,2,128,256]{5,4,3,2,1,0:T(8,128)(2,1)S(1)}, bf16[4,4,2,2,128,256]{5,4,3,2,1,0:T(8,128)(2,1)}, u32[]{:S(2)}) copy-start(bf16[4,4,2,2,128,256]{5,4,3,2,1,0:T(8,128)(2,1)} %copy-done.6) | copy-start | bytes 12582916 | tf_op jit(solution)/shard_map/cond
  101.3 12.3 %copy-start.49 = (bf16[1,88,2048]{2,1,0:T(8,128)(2,1)S(1)}, bf16[1,88,2048]{2,1,0:T(8,128)(2,1)}, u32[]{:S(2)}) copy-start(bf16[1,88,2048]{2,1,0:T(8,128)(2,1)} %get-tuple-element.235) | copy-start | bytes 1081348 | tf_op jit(solution)/shard_map/cond
  101.3 12.3 %copy-start.57 = (bf16[1,88,2048]{2,1,0:T(8,128)(2,1)S(1)}, bf16[1,88,2048]{2,1,0:T(8,128)(2,1)}, u32[]{:S(2)}) copy-start(bf16[1,88,2048]{2,1,0:T(8,128)(2,1)} %get-tuple-element.236) | copy-start | bytes 1081348 | tf_op jit(solution)/shard_map/cond
  101.3 12.3 %copy-start.62 = (bf16[1,88,2048]{2,1,0:T(8,128)(2,1)S(1)}, bf16[1,88,2048]{2,1,0:T(8,128)(2,1)}, u32[]{:S(2)}) copy-start(bf16[1,88,2048]{2,1,0:T(8,128)(2,1)} %get-tuple-element.237) | copy-start | bytes 1081348 | tf_op jit(solution)/shard_map/cond
  101.3 12.3 %copy-start.67 = (bf16[1,88,2048]{2,1,0:T(8,128)(2,1)S(1)}, bf16[1,88,2048]{2,1,0:T(8,128)(2,1)}, u32[]{:S(2)}) copy-start(bf16[1,88,2048]{2,1,0:T(8,128)(2,1)} %get-tuple-element.238) | copy-start | bytes 1081348 | tf_op jit(solution)/shard_map/cond
  101.3 12.3 %copy-start.72 = (bf16[1,88,2048]{2,1,0:T(8,128)(2,1)S(1)}, bf16[1,88,2048]{2,1,0:T(8,128)(2,1)}, u32[]{:S(2)}) copy-start(bf16[1,88,2048]{2,1,0:T(8,128)(2,1)} %get-tuple-element.239) | copy-start | bytes 1081348 | tf_op jit(solution)/shard_map/cond
  101.3 12.3 %copy-start.77 = (bf16[1,88,2048]{2,1,0:T(8,128)(2,1)S(1)}, bf16[1,88,2048]{2,1,0:T(8,128)(2,1)}, u32[]{:S(2)}) copy-start(bf16[1,88,2048]{2,1,0:T(8,128)(2,1)} %get-tuple-element.240) | copy-start | bytes 1081348 | tf_op jit(solution)/shard_map/cond
  101.3 12.3 %copy-start.82 = (bf16[1,88,2048]{2,1,0:T(8,128)(2,1)S(1)}, bf16[1,88,2048]{2,1,0:T(8,128)(2,1)}, u32[]{:S(2)}) copy-start(bf16[1,88,2048]{2,1,0:T(8,128)(2,1)} %get-tuple-element.241) | copy-start | bytes 1081348 | tf_op jit(solution)/shard_map/cond
  101.4 12.3 %copy-start.86 = (bf16[1,88,2048]{2,1,0:T(8,128)(2,1)S(1)}, bf16[1,88,2048]{2,1,0:T(8,128)(2,1)}, u32[]{:S(2)}) copy-start(bf16[1,88,2048]{2,1,0:T(8,128)(2,1)} %get-tuple-element.242) | copy-start | bytes 1081348 | tf_op jit(solution)/shard_map/cond
  101.4 12.3 %copy-start.90 = (bf16[1,88,2048]{2,1,0:T(8,128)(2,1)S(1)}, bf16[1,88,2048]{2,1,0:T(8,128)(2,1)}, u32[]{:S(2)}) copy-start(bf16[1,88,2048]{2,1,0:T(8,128)(2,1)} %get-tuple-element.243) | copy-start | bytes 1081348 | tf_op jit(solution)/shard_map/cond
  111.8 1.0 copy-start.18
  112.8 0.8 copy-start.40
  124.4 0.8 copy-start.32
  125.2 10.7 %collective-permute-start.29 = (bf16[4,4,2,2,128,256]{5,4,3,2,1,0:T(8,128)(2,1)}, bf16[4,4,2,2,128,256]{5,4,3,2,1,0:T(8,128)(2,1)S(1)}, u32[]{:S(2)}, u32[]{:S(2)}) collective-permute-start(bf16[4,4,2,2,128,256]{5,4,3,2,1,0:T(8,128)(2,1)} %all-to-all-done.19.refs_5_), channel_id=1, source_target_pairs={{0,8},{8,0},{1,9},{9,1},{2,10},{10,2},{3,11},{11,3},{4,12},{12,4},... | collective-permute-start | bytes 12582920 | tf_op jit(solution)/shard_map/cond/branch_4_fun/ppermute | solution.py:231
  129.8 25.7 %copy-start.19 = (f32[3,40,2048]{2,1,0:T(8,128)S(1)}, f32[3,40,2048]{2,1,0:T(8,128)}, u32[]{:S(2)}) copy-start(f32[3,40,2048]{2,1,0:T(8,128)} %copy-done.18) | copy-start | bytes 2949124 | tf_op jit(solution)/shard_map/cond
  135.9 1.1 copy-start.33
  137.0 18.6 %copy-start.41 = (bf16[3,40,2048]{2,1,0:T(8,128)(2,1)S(1)}, bf16[3,40,2048]{2,1,0:T(8,128)(2,1)}, u32[]{:S(2)}) copy-start(bf16[3,40,2048]{2,1,0:T(8,128)(2,1)} %copy-done.40) | copy-start | bytes 1474564 | tf_op jit(solution)/shard_map/cond
  146.2 28.0 %collective-permute-start.30 = (bf16[3,48,2048]{2,1,0:T(8,128)(2,1)S(1)}, bf16[3,48,2048]{2,1,0:T(8,128)(2,1)S(1)}, u32[]{:S(2)}, u32[]{:S(2)}) collective-permute-start(bf16[3,48,2048]{2,1,0:T(8,128)(2,1)S(1)} %adam_step.34), channel_id=1, source_target_pairs={{64,0},{128,64},{192,128},{256,192},{320,256},{384,320},{448,384},... | collective-permute-start | bytes 1769480 | tf_op jit(solution)/shard_map/cond/branch_4_fun/ppermute | solution.py:207
  165.0 19.2 %collective-permute-start.31 = (bf16[3,40,2048]{2,1,0:T(8,128)(2,1)S(1)}, bf16[3,40,2048]{2,1,0:T(8,128)(2,1)S(1)}, u32[]{:S(2)}, u32[]{:S(2)}) collective-permute-start(bf16[3,40,2048]{2,1,0:T(8,128)(2,1)S(1)} %adam_step.35), channel_id=1, source_target_pairs={{64,0},{128,64},{192,128},{256,192},{320,256},{384,320},{448,384},... | collective-permute-start | bytes 1474568 | tf_op jit(solution)/shard_map/cond/branch_4_fun/ppermute | solution.py:207
